TPU v7x, 128 devices: a whole 4x4x4 slice. The times are simulated.
128 devices in a mesh: sub: 16 (over y, z), corner: 8 (over x, core).
Axes of the slice: x: 4, y: 4, z: 4, core: 2. Of those that a mesh axis runs over, the one named last changes fastest.
Arguments:
- right_side: float32 [2048, 64, 128], P(('sub', 'corner'))
- diagonal: float32 [2048, 64], P(('sub', 'corner')), may hold values from 1.25 to 2.5
- stiffness: float32 [2048, 64, 192], P(('sub', 'corner')), may hold values from -0.035721725 to 0.035721725
- column_index: int32 [2048, 3], P(('sub', 'corner')), may hold values from 0 to 15, as said below
- neighbours: int32 [128, 8], P(('sub', 'corner')), may hold values from 0 to 15, as said below
- face_count: int32 [128, 8], P(('sub', 'corner')), may hold values from 1 to 2, as said below
- corner_group: int32 [128, 8], P(('sub', 'corner')), may hold values from 0 to 15
- coarse_inverse: float32 [1024, 1024], P('corner'), as said below
Outputs:
- solution: float32 [2048, 64, 128], P(('sub', 'corner'))
- residual: float32 [2048, 64, 128], P(('sub', 'corner'))
Inputs may be any that keep to these rules, and one draw needn't show every extreme that they name: `neighbours`: for each round r < 8 and corner index c, the subdomains s * 8 + c pair up: if the entry of s is p, then p differs from s and the entry of p in round r is s; the rounds of one subdomain name different partners. `face_count`: equal on both sides of a pair in a round; in every round and corner index some pair shares 2 blocks. `column_index`: the 3 entries of a block row name blocks of the same subdomain other than the row's own, all different; for each k < 3, entry k over the 16 rows of one subdomain names each of its blocks exactly once. `coarse_inverse`: symmetric and positive definite.
All inputs are finite; a program needn't handle non-finite values.
Results may differ from a plain program's by a relative error of at most 0.0003.
Values sent between devices are 32-bit elements; how exact they have to be, the bound alone decides.
No kernel may reach another device: no remote copies, remote signals or barrier semaphores. Data moves between devices by JAX's collectives and lax.ppermute only.
A program may use at most 128 MiB of HBM per device.

v0:
```python
import jax
import jax.numpy as jnp
from jax import lax
from jax.sharding import PartitionSpec as P

FMAX = 2
NG = 16
DEGREE = 8
ITERS = 3


CENTER_VALUE = 1.0
HALF_RANGE = 0.8
PENALTY = 1.0
HIGHEST_PRECISION = lax.Precision.HIGHEST


def local_product(stiffness, column_index, inverse_index, link_index, vector):
    blocks = vector.shape[0]
    picked = vector[column_index].reshape(blocks, -1, vector.shape[2])
    forward = jnp.einsum("bij,bjr->bir", stiffness, picked, precision=HIGHEST_PRECISION)
    backward = jnp.einsum("bij,bir->bjr", stiffness, vector, precision=HIGHEST_PRECISION)
    backward = backward.reshape(blocks, -1, vector.shape[1], vector.shape[2])
    spread = jnp.sum(backward[inverse_index, link_index[None, :]], axis=1)
    return forward + spread


def on_device(
    right_side,
    diagonal,
    stiffness,
    column_index,
    neighbours,
    face_count,
    corner_group,
    coarse_inverse,
):
    blocks = right_side.shape[0]
    block_width = right_side.shape[1]
    load_count = right_side.shape[2]
    rounds = neighbours.shape[1]
    corners = corner_group.shape[1]
    inverse_index = jnp.argsort(column_index, axis=0)
    link_index = jnp.arange(column_index.shape[1], dtype=jnp.int32)
    scale_diag = diagonal[:, :, None]
    peer_subs = neighbours[0]
    round_ids = jnp.arange(rounds, dtype=jnp.int32)
    face_mask = (jnp.arange(FMAX, dtype=jnp.int32)[None, :] < face_count[0][:, None])[
        :, :, None, None
    ]
    selector = (corner_group[0][:, None] == jnp.arange(NG, dtype=jnp.int32)[None, :]).astype(
        jnp.float32
    )
    face_extent = rounds * FMAX

    def stiffness_apply(vector):
        return scale_diag * vector + local_product(
            stiffness, column_index, inverse_index, link_index, vector
        )

    def chebyshev(source):
        sigma_ratio = CENTER_VALUE / HALF_RANGE
        residual = source
        solution = jnp.zeros_like(source)
        direction = residual / (CENTER_VALUE * scale_diag)
        ratio_now = 1.0 / sigma_ratio
        for degree in range(DEGREE):
            solution = solution + direction
            if degree + 1 < DEGREE:
                residual = residual - stiffness_apply(direction)
                ratio_next = 1.0 / (2.0 * sigma_ratio - ratio_now)
                direction = (
                    ratio_next * ratio_now * direction
                    + 2.0 * ratio_next / HALF_RANGE * residual / scale_diag
                )
                ratio_now = ratio_next
        return solution

    def coarse_term(vector):
        corner_rows = vector[blocks - corners :]
        partial_sum = jnp.einsum("cg,cir->gir", selector, corner_rows, precision=HIGHEST_PRECISION)
        totals = lax.psum(partial_sum.reshape(NG * block_width, load_count), ("sub", "corner"))
        owned_rows = jnp.dot(
            coarse_inverse, totals, precision=HIGHEST_PRECISION, preferred_element_type=jnp.float32
        )
        coarse = lax.all_gather(owned_rows, "corner", axis=0, tiled=True).reshape(
            NG, block_width, load_count
        )
        return jnp.einsum("cg,gir->cir", selector, coarse, precision=HIGHEST_PRECISION)

    def precondition(vector):
        return chebyshev(vector).at[blocks - corners :].add(coarse_term(vector))

    def column_dot(first_vector, second_vector):
        return jnp.sum(first_vector * second_vector, axis=(0, 1))

    def progress(residual, corrected):
        return lax.psum(column_dot(residual, corrected), ("sub", "corner"))

    residual = right_side
    solution = jnp.zeros_like(right_side)
    corrected = precondition(residual)
    direction = corrected
    energy_now = progress(residual, corrected)
    for iteration in range(ITERS):
        apply_face_rows = direction.reshape(rounds, FMAX, block_width, load_count)
        collected = lax.all_gather(apply_face_rows[None], "sub", axis=0, tiled=True)
        coupling = PENALTY * jnp.where(
            face_mask, apply_face_rows - collected[peer_subs, round_ids], 0.0
        )
        mapped = (
            stiffness_apply(direction)
            .at[:face_extent]
            .add(coupling.reshape(face_extent, block_width, load_count))
        )
        curvature = lax.psum(column_dot(direction, mapped), ("sub", "corner"))
        step_size = energy_now / curvature
        solution = solution + step_size * direction
        residual = residual - step_size * mapped
        if iteration + 1 < ITERS:
            corrected = precondition(residual)
            energy_next = progress(residual, corrected)
            direction = corrected + energy_next / energy_now * direction
            energy_now = energy_next
    return (solution, residual)


def solution(mesh):
    placed = (
        P(("sub", "corner"), None, None),
        P(("sub", "corner"), None),
        P(("sub", "corner"), None, None),
        P(("sub", "corner"), None),
        P(("sub", "corner"), None),
        P(("sub", "corner"), None),
        P(("sub", "corner"), None),
        P("corner", None),
    )
    return jax.shard_map(
        on_device,
        mesh=mesh,
        in_specs=placed,
        out_specs=(P(("sub", "corner"), None, None), P(("sub", "corner"), None, None)),
        check_vma=False,
    )
```

profile of v0, /device:TPU:1, one launch (start us, length us, event | category | flops | bytes accessed | tf_op | source)
XLA Modules:
  0.0 1284.2 jit_solution(17289549467420094888)
XLA Ops:
  12.0 4.0 fusion.121
  35.0 4.1 divide_add_fusion.16
  41.0 4.0 fusion.125
  63.2 4.2 divide_add_fusion.14
  69.2 3.8 fusion.127
  78.8 4.6 divide_add_fusion.13
  94.8 4.4 divide_add_fusion.12
  112.5 4.4 fusion.24
  116.9 44.4 %all-reduce.5.cloned.1.call-done = f32[1024,128]{1,0:T(8,128)} async-done(((f32[1024,128]{1,0:T(8,128)}), f32[1024,128]{1,0:T(8,128)}) %all-reduce.5.cloned.1.call-update) | async-done | bytes 524304 | tf_op jit(solution)/shard_map/psum | solution.py:82
  163.5 13.4 %all_gather.18 = f32[1024,128]{0,1:T(8,128)S(1)} all-gather(f32[128,128]{0,1:T(8,128)S(1)} %convolution_bitcast_fusion.26), channel_id=1, replica_groups=mesh['sub'=16,'corner'=8] {'corner'}, dimensions={0}, use_global_device_ids=true | all-gather | bytes 589824 | tf_op jit(solution)/shard_map/all_gather | solution.py:86
  181.9 3.8 fusion.130
  189.0 58.2 %all-gather.4.cloned.1.call-done = f32[16,8,2,64,128]{4,3,2,1,0:T(8,128)} async-done(((f32[1,8,2,64,128]{4,3,2,1,0:T(8,128)}), f32[16,8,2,64,128]{4,3,2,1,0:T(8,128)}) %all-gather.4.cloned.1.call-update) | async-done | bytes 8388624 | tf_op jit(solution)/shard_map/all_gather | solution.py:107
  247.2 4.8 gather_fusion.16
  256.3 64.7 %all-reduce = (f32[128]{0:T(128)S(1)}, f32[128]{0:T(128)S(1)}) all-reduce(f32[128]{0:T(128)S(1)} %get-tuple-element.101, f32[128]{0:T(128)S(1)} %get-tuple-element.100), channel_id=1, replica_groups=mesh['sub'=16,'corner'=8] {'sub','corner'}, use_global_device_ids=true, to_apply=%region_10.11 | all-reduce | flops 256 | bytes 2048 | tf_op jit(solution)/shard_map/psum | solution.py:98
  322.3 4.0 fusion.122
  333.1 4.1 divide_add_fusion.11
  354.1 4.0 fusion.132
  363.9 4.2 divide_add_fusion.9
  379.5 4.4 divide_add_fusion.8
  395.3 5.0 divide_add_fusion.7
  403.1 4.9 fusion.135
  413.8 4.6 divide_add_fusion.6
  433.4 5.2 fusion.52
  438.6 131.4 %all-reduce.7.cloned.1.call-done = f32[1024,128]{1,0:T(8,128)} async-done(((f32[1024,128]{1,0:T(8,128)}), f32[1024,128]{1,0:T(8,128)}) %all-reduce.7.cloned.1.call-update) | async-done | bytes 524304 | tf_op jit(solution)/shard_map/psum | solution.py:82
  572.2 13.1 %all_gather.20 = f32[1024,128]{0,1:T(8,128)S(1)} all-gather(f32[128,128]{0,1:T(8,128)S(1)} %convolution_bitcast_fusion.25), channel_id=1, replica_groups=mesh['sub'=16,'corner'=8] {'corner'}, dimensions={0}, use_global_device_ids=true | all-gather | bytes 589824 | tf_op jit(solution)/shard_map/all_gather | solution.py:86
  588.2 63.7 %psum.67 = f32[128]{0:T(128)S(1)} all-reduce(f32[128]{0:T(128)S(1)} %multiply_reduce_fusion.3), channel_id=1, replica_groups=mesh['sub'=16,'corner'=8] {'sub','corner'}, use_global_device_ids=true, to_apply=%region_23.24 | all-reduce | flops 128 | bytes 1024 | tf_op jit(solution)/shard_map/psum | solution.py:98
  655.6 3.8 fusion.137
  664.6 55.8 %all-gather.6.cloned.1.call-done = f32[16,8,2,64,128]{4,3,2,1,0:T(8,128)} async-done(((f32[1,8,2,64,128]{4,3,2,1,0:T(8,128)}), f32[16,8,2,64,128]{4,3,2,1,0:T(8,128)}) %all-gather.6.cloned.1.call-update) | async-done | bytes 8388624 | tf_op jit(solution)/shard_map/all_gather | solution.py:107
  720.4 4.8 gather_fusion.33
  729.4 64.9 %psum.68 = f32[128]{0:T(128)S(1)} all-reduce(f32[128]{0:T(128)S(1)} %get-tuple-element.135), channel_id=1, replica_groups=mesh['sub'=16,'corner'=8] {'sub','corner'}, use_global_device_ids=true, to_apply=%region_26.27 | all-reduce | flops 128 | bytes 1024 | tf_op jit(solution)/shard_map/psum | solution.py:116
  795.7 4.0 fusion.123
  807.3 4.2 divide_add_fusion.5
  823.0 4.4 divide_add_fusion.4
  829.2 4.0 fusion.139
  838.9 4.4 divide_add_fusion.3
  854.7 4.6 divide_add_fusion.2
  862.1 4.9 fusion.141
  872.8 4.9 divide_add_fusion.1
  880.6 4.9 fusion.142
  891.2 4.5 divide_add_fusion
  910.8 5.3 fusion.80
  916.2 131.2 %all-reduce.9.cloned.1.call-done = f32[1024,128]{1,0:T(8,128)} async-done(((f32[1024,128]{1,0:T(8,128)}), f32[1024,128]{1,0:T(8,128)}) %all-reduce.9.cloned.1.call-update) | async-done | bytes 524304 | tf_op jit(solution)/shard_map/psum | solution.py:82
  1049.6 14.2 %all_gather.22 = f32[1024,128]{0,1:T(8,128)} all-gather(f32[128,128]{0,1:T(8,128)S(1)} %convolution_bitcast_fusion.24), channel_id=1, replica_groups=mesh['sub'=16,'corner'=8] {'corner'}, dimensions={0}, use_global_device_ids=true | all-gather | bytes 589824 | tf_op jit(solution)/shard_map/all_gather | solution.py:86
  1067.8 63.7 %psum.70 = f32[128]{0:T(128)S(1)} all-reduce(f32[128]{0:T(128)S(1)} %multiply_reduce_fusion.1), channel_id=1, replica_groups=mesh['sub'=16,'corner'=8] {'sub','corner'}, use_global_device_ids=true, to_apply=%region_36.37 | all-reduce | flops 128 | bytes 1024 | tf_op jit(solution)/shard_map/psum | solution.py:98
  1135.3 3.8 fusion.144
  1145.0 55.0 %all-gather.8.cloned.1.call-done = f32[16,8,2,64,128]{4,3,2,1,0:T(8,128)} async-done(((f32[1,8,2,64,128]{4,3,2,1,0:T(8,128)}), f32[16,8,2,64,128]{4,3,2,1,0:T(8,128)}) %all-gather.8.cloned.1.call-update) | async-done | bytes 8388624 | tf_op jit(solution)/shard_map/all_gather | solution.py:107
  1200.0 4.8 gather_fusion.50
  1210.1 64.5 %psum.71 = f32[128]{0:T(128)S(1)} all-reduce(f32[128]{0:T(128)S(1)} %get-tuple-element.149), channel_id=1, replica_groups=mesh['sub'=16,'corner'=8] {'sub','corner'}, use_global_device_ids=true, to_apply=%region_39.40 | all-reduce | flops 128 | bytes 1024 | tf_op jit(solution)/shard_map/psum | solution.py:116
  (212 shorter events, 281.0 us)
Async XLA Ops:
  7.2 4.8 copy-start
  7.2 4.6 copy-start.12
  7.2 3.4 copy-start.27
  7.2 4.6 copy-start.24
  7.2 154.1 %all-reduce.5.cloned.1.call-start = ((), (), s32[]{:S(2)}) async-start(), calls=%async_computation | async-start | bytes 1048576 | tf_op jit(solution)/shard_map/psum | solution.py:82
  10.5 236.7 %all-gather.4.cloned.1.call-start = ((), (), s32[]{:S(2)}) async-start(), calls=%async_computation.1 | async-start | bytes 8912896 | tf_op jit(solution)/shard_map/all_gather | solution.py:107
  24.4 10.6 copy-start.8
  83.4 11.4 copy-start.5
  99.2 0.8 copy-start.11
  116.9 60.3 %copy-start.26 = (s32[1,8]{1,0:T(1,128)S(1)}, s32[1,8]{1,0:T(1,128)}, u32[]{:S(2)}) copy-start(s32[1,8]{1,0:T(1,128)} %param.32) | copy-start | bytes 100
  177.0 1.8 copy-start.28
  177.0 2.0 copy-start.29
  177.9 0.8 copy-start.1
  178.7 391.3 %all-reduce.7.cloned.1.call-start = ((), (), s32[]{:S(2)}) async-start(), calls=%async_computation.2 | async-start | bytes 1048576 | tf_op jit(solution)/shard_map/psum | solution.py:82
  178.9 3.0 copy-start.2
  189.0 64.3 %copy-start.13 = (f32[16,64,128]{2,1,0:T(8,128)S(1)}, f32[16,64,128]{2,1,0:T(8,128)}, u32[]{:S(2)}) copy-start(f32[16,64,128]{2,1,0:T(8,128)} %param.26) | copy-start | bytes 1572868
  189.0 64.3 %copy-start.25 = (f32[16,64,128]{2,1,0:T(8,128)S(1)}, f32[16,64,128]{2,1,0:T(8,128)}, u32[]{:S(2)}) copy-start(f32[16,64,128]{2,1,0:T(8,128)} %reduce_sum.278) | copy-start | bytes 1572868
  252.0 1.6 copy-start.23
  322.3 10.8 copy-start.14
  337.3 11.4 copy-start.6
  418.4 0.8 copy-start.9
  427.4 293.0 %all-gather.6.cloned.1.call-start = ((), (), s32[]{:S(2)}) async-start(), calls=%async_computation.3 | async-start | bytes 8912896 | tf_op jit(solution)/shard_map/all_gather | solution.py:107
  438.6 149.4 %copy-start.19 = (f32[16,64,128]{2,1,0:T(8,128)S(1)}, f32[16,64,128]{2,1,0:T(8,128)}, u32[]{:S(2)}) copy-start(f32[16,64,128]{2,1,0:T(8,128)} %fusion.52) | copy-start | bytes 1572868
  572.2 15.9 %copy-start.15 = (f32[16,64,128]{2,1,0:T(8,128)S(1)}, f32[16,64,128]{2,1,0:T(8,128)}, u32[]{:S(2)}) copy-start(f32[16,64,128]{2,1,0:T(8,128)} %copy-done.14) | copy-start | bytes 1572868
  652.7 1.0 copy-start.3
  652.7 394.7 %all-reduce.9.cloned.1.call-start = ((), (), s32[]{:S(2)}) async-start(), calls=%async_computation.4 | async-start | bytes 1048576 | tf_op jit(solution)/shard_map/psum | solution.py:82
  725.1 1.6 copy-start.22
  795.7 4.0 copy-start.16
  804.9 2.4 copy-start.17
  811.6 11.4 copy-start.7
  895.7 0.8 copy-start.10
  904.7 295.3 %all-gather.8.cloned.1.call-start = ((), (), s32[]{:S(2)}) async-start(), calls=%async_computation.5 | async-start | bytes 8912896 | tf_op jit(solution)/shard_map/all_gather | solution.py:107
  916.2 151.4 %copy-start.20 = (f32[16,64,128]{2,1,0:T(8,128)S(1)}, f32[16,64,128]{2,1,0:T(8,128)}, u32[]{:S(2)}) copy-start(f32[16,64,128]{2,1,0:T(8,128)} %fusion.80) | copy-start | bytes 1572868
  1049.6 18.0 %copy-start.18 = (f32[16,64,128]{2,1,0:T(8,128)S(1)}, f32[16,64,128]{2,1,0:T(8,128)}, u32[]{:S(2)}) copy-start(f32[16,64,128]{2,1,0:T(8,128)} %copy-done.16) | copy-start | bytes 1572868
  1132.3 1.0 copy-start.4
  1204.8 1.6 copy-start.21
Sparse Core Ops, SparseCore 0:
  12.8 148.5 all-reduce.4
  178.8 68.3 all-gather.3
  427.5 142.4 all-reduce.6
  652.9 67.4 all-gather.5
  904.9 142.5 all-reduce.8
  1132.5 67.4 all-gather.7
where the time goes:
time: 1300 us; the launch traced here: 1280 us
  waiting for transfers between devices  476 us (37%)
  blocking collectives  362 us (28%)
  matrix products  210 us (16%)
  local copies, waits for them, and re-layouts  157 us (12%)
  other arithmetic  62.6 us (5%)
  between operations  15.1 us (1%)
    psum x3, waiting for transfers between devices, coarse_term(): lax.psum(partial_sum.reshape(NG * block_width, load_count), ('sub', 'corn...  307 us
    psum x3, blocking collectives, progress(): return lax.psum(column_dot(residual, corrected), ('sub', 'corner'))  192 us
    all_gather x3, waiting for transfers between devices, on_device(): collected = lax.all_gather(apply_face_rows[None], 'sub', axis=0, tiled=True)  169 us
    psum x2, blocking collectives, on_device(): curvature = lax.psum(column_dot(direction, mapped), ('sub', 'corner'))  129 us
    dot_general x24, matrix products, local_product(): jnp.einsum('bij,bjr->bir', stiffness, picked, precision=HIGHEST_PRECISION)  102 us
    dot_general x24, matrix products, local_product(): jnp.einsum('bij,bir->bjr', stiffness, vector, precision=HIGHEST_PRECISION)  95.8 us
    gather x24, local copies, waits for them, and re-layouts, local_product(): spread = jnp.sum(backward[inverse_index, link_index[None, :]], axis=1)  78.5 us
    gather x24, local copies, waits for them, and re-layouts, local_product(): picked = vector[column_index].reshape(blocks, -1, vector.shape[2])  50.8 us
  transfers between devices with their start and end apart: 6, of which 6 were waited for; matrix products, arithmetic and copies ran while one was open for 12% of the time, Pallas kernels for 0%

commit v1 on v0

v1 whole, which is shorter than its diff:
```python
import functools

import jax
import jax.numpy as jnp
from jax import lax
from jax.experimental import pallas as pl
from jax.experimental.pallas import tpu as pltpu
from jax.sharding import PartitionSpec as P

F32 = jnp.float32
BF16 = jnp.bfloat16
BLOCK = 64
NB = 16
DOF = NB * BLOCK
RHS = 128
BW = 3
NG = 16
NCB = 8
ROUNDS = 8
DEGREE = 8
HALF_RANGE = 0.8
SIGMA = 1.0 / HALF_RANGE
CHUNK = 128
EXTRA = 8
HEAD = CHUNK + EXTRA
SLOT = HEAD + 2 * BLOCK
TILE = 256
SPLIT = 4
VMEM_LIMIT = 48 * 1024 * 1024


def spec(kind):
    return pl.BlockSpec(memory_space=pltpu.SMEM if kind == "s" else pltpu.VMEM)


def call(body, name, kinds, out_kinds, outs, scratch=(), flops=0):
    return pl.pallas_call(
        body,
        name=name,
        in_specs=[spec(k) for k in kinds],
        out_specs=tuple(spec(k) for k in out_kinds),
        out_shape=tuple(jax.ShapeDtypeStruct(s, t) for s, t in outs),
        scratch_shapes=list(scratch),
        compiler_params=pltpu.CompilerParams(vmem_limit_bytes=VMEM_LIMIT),
        cost_estimate=pl.CostEstimate(
            flops=flops, bytes_accessed=4 * 1024 * 1024, transcendentals=0
        ),
    )


def tiles():
    return [slice(i, i + TILE) for i in range(0, DOF, TILE)]


def put_split(pair, rows, value):
    high = value.astype(BF16)
    pair[rows, :RHS] = high
    pair[rows, RHS:] = (value - high.astype(F32)).astype(BF16)


def product(high, low, pair, rows):
    both = jnp.dot(high[rows, :], pair[...], preferred_element_type=F32)
    rest = jnp.dot(low[rows, :], pair[:, :RHS], preferred_element_type=F32)
    return both[:, :RHS] + (both[:, RHS:] + rest)


def build_kernel(column, stiffness, scale, high, low, inverse, total):
    total[...] = jnp.zeros_like(total)
    lane_half = lax.broadcasted_iota(jnp.int32, (BLOCK, 2 * BLOCK), 1) // BLOCK
    for row in range(NB):
        for link in range(BW):
            part = stiffness[row, :, link * BLOCK : (link + 1) * BLOCK]
            turned = part.T
            target = column[row, link]
            offset = pl.multiple_of((target // 2) * 2 * BLOCK, 2 * BLOCK)
            rows = slice(row * BLOCK, (row + 1) * BLOCK)
            total[rows, pl.ds(offset, 2 * BLOCK)] += jnp.where(
                lane_half == target % 2, jnp.concatenate([part, part], axis=1), 0.0
            )
            lanes = slice((row // 2) * 2 * BLOCK, (row // 2 + 1) * 2 * BLOCK)
            below = pl.ds(pl.multiple_of(target * BLOCK, BLOCK), BLOCK)
            total[below, lanes] += jnp.where(
                lane_half == row % 2, jnp.concatenate([turned, turned], axis=1), 0.0
            )
    for rows in tiles():
        value = total[rows, :]
        top = value.astype(BF16)
        high[rows, :] = top
        low[rows, :] = (value - top.astype(F32)).astype(BF16)
    inverse[...] = 1.0 / scale[...]


def split_kernel(value, high, low):
    for rows in tiles():
        part = value[rows, :]
        top = part.astype(BF16)
        high[rows, :] = top
        low[rows, :] = (part - top.astype(F32)).astype(BF16)


def restrict_into(groups, place, vector, extra, bins, away, keep):
    bins[...] = jnp.zeros_like(bins)
    for corner in range(NCB):
        group = groups[0, corner]
        apart = (group // 2) ^ place[0]
        slot = (apart & 1) * 4 + (apart & 2) + ((apart >> 2) & 1)
        rows = pl.ds(pl.multiple_of((group % 2) * BLOCK, BLOCK), BLOCK)
        first = (NB - NCB + corner) * BLOCK
        bins[slot, rows, :] += vector[first : first + BLOCK, :]
    if extra is not None:
        for slot in range(NCB):
            bins[slot, CHUNK:, :] = extra
    keep[...] = bins[:4]
    away[...] = bins[4:]


def restrict_kernel(groups, place, vector, away, keep, bins):
    restrict_into(groups, place, vector, None, bins, away, keep)


def chebyshev_steps(first, last, scale, inverse, high, low, x, h, e, pairs):
    ratio = 1.0 / SIGMA
    for step in range(last):
        later = 1.0 / (2.0 * SIGMA - ratio)
        if step >= first:
            for rows in tiles():
                now = e[rows, :]
                image = product(high, low, pairs.at[step % 2], rows)
                x[rows, :] = now if step == 0 else x[rows, :] + now
                left = h[rows, :] - (scale[rows, :] * now + image)
                h[rows, :] = left
                new = (later * ratio) * now + (2.0 * later / HALF_RANGE) * (
                    left * inverse[rows, :]
                )
                e[rows, :] = new
                if step + 1 < last:
                    put_split(pairs.at[(step + 1) % 2], rows, new)
        ratio = later


def chebyshev_first(source, scale, inverse, high, low, x, h, e, pairs):
    for rows in tiles():
        value = source[rows, :]
        h[rows, :] = value
        value = value * inverse[rows, :]
        e[rows, :] = value
        put_split(pairs.at[0], rows, value)
    chebyshev_steps(0, SPLIT, scale, inverse, high, low, x, h, e, pairs)


def chebyshev_last(
    with_groups, peers, scale, inverse, high, low, x0, h0, e0, kept, came1, came2, came3, extra,
    y, send, h, e, pairs,
):
    y[...] = x0[...]
    h[...] = h0[...]
    e[...] = e0[...]
    for rows in tiles():
        put_split(pairs.at[SPLIT % 2], rows, e0[rows, :])
    chebyshev_steps(SPLIT, DEGREE - 1, scale, inverse, high, low, y, h, e, pairs)
    y[...] += e[...]
    head = kept[0] + came1[0] + (came2[0] + came3[0])
    for slot in range(NB):
        send[slot, :HEAD, :] = head
        if with_groups:
            send[slot, CHUNK:HEAD, :] = extra[...]
        send[slot, HEAD:, :] = jnp.zeros((2 * BLOCK, RHS), F32)
    for turn in range(ROUNDS):
        send[peers[0, turn], HEAD:, :] = y[turn * 2 * BLOCK : (turn + 1) * 2 * BLOCK, :]


def gather_kernel(received, total, dots):
    value = received[0, :HEAD, :]
    for slot in range(1, NB):
        value = value + received[slot, :HEAD, :]
    total[...] = value[:CHUNK]
    dots[...] = value[CHUNK:]


def column_dot(pairs_of):
    total = None
    for first, second in pairs_of:
        part = jnp.sum(
            (first * second).reshape(first.shape[0] // 8, 8, RHS), axis=0
        )
        total = part if total is None else total + part
    return jnp.sum(total, axis=0, keepdims=True)


def apply_all(
    groups, peers, counts, others, received, y, totals, cih, cil, high, low, scale,
    m, n, coarse, pair,
):
    for rows in tiles():
        put_split(pair, rows, totals[rows, :])
    for rows in tiles():
        coarse[rows, :] = product(cih, cil, pair, rows)

    def block_of(group):
        return coarse[pl.ds(pl.multiple_of(group * BLOCK, BLOCK), BLOCK), :]

    half = (NB - NCB) * BLOCK
    m[:half, :] = y[:half, :]
    for corner in range(NCB):
        rows = slice(half + corner * BLOCK, half + (corner + 1) * BLOCK)
        m[rows, :] = y[rows, :] + block_of(groups[0, corner])
    for rows in tiles():
        put_split(pair, rows, m[rows, :])
    for rows in tiles():
        n[rows, :] = scale[rows, :] * m[rows, :] + product(high, low, pair, rows)
    for block in range(2 * ROUNDS):
        turn, side = block // 2, block % 2
        rows = slice(block * BLOCK, (block + 1) * BLOCK)
        first = HEAD + side * BLOCK
        other = received[peers[0, turn], first : first + BLOCK, :]
        if block >= NB - NCB:
            other = other + block_of(others[0, block - (NB - NCB)])
        n[rows, :] += jnp.where(side < counts[0, turn], m[rows, :] - other, 0.0)


def stage0_kernel(
    groups, place, peers, counts, received, y, totals, cih, cil, high, low, scale, b,
    u, w, away, keep, others, coarse, pair, bins,
):
    lanes = lax.broadcasted_iota(jnp.int32, (1, RHS), 1)
    for corner in range(NCB):
        row = received[peers[0, (NB - NCB + corner) // 2], CHUNK : CHUNK + 1, :]
        picked = jnp.sum(jnp.where(lanes == corner, row, 0.0))
        others[0, corner] = picked.astype(jnp.int32)
    apply_all(
        groups, peers, counts, others, received, y, totals, cih, cil, high, low, scale,
        u, w, coarse, pair,
    )
    energy = column_dot([(b[r, :], u[r, :]) for r in tiles()])
    curve = column_dot([(w[r, :], u[r, :]) for r in tiles()])
    extra = jnp.concatenate([energy, curve, jnp.zeros((EXTRA - 2, RHS), F32)], axis=0)
    restrict_into(groups, place, w, extra, bins, away, keep)


def stage1_kernel(
    groups, place, peers, counts, others, received, y, totals, cih, cil, high, low, scale, b,
    dots, u0, w0,
    m, n, u, w, away, keep, scalars, coarse, pair, bins,
):
    apply_all(
        groups, peers, counts, others, received, y, totals, cih, cil, high, low, scale,
        m, n, coarse, pair,
    )
    energy, curve = dots[0:1, :], dots[1:2, :]
    step = energy / curve
    scalars[...] = jnp.concatenate(
        [energy, curve, step, jnp.zeros((EXTRA - 3, RHS), F32)], axis=0
    )
    for r in tiles():
        u[r, :] = u0[r, :] - step * m[r, :]
        w[r, :] = w0[r, :] - step * n[r, :]
    new_energy = column_dot([(b[r, :] - step * w0[r, :], u[r, :]) for r in tiles()])
    new_curve = column_dot([(w[r, :], u[r, :]) for r in tiles()])
    cross = column_dot(
        [(u[r, :], w0[r, :]) for r in tiles()] + [(u0[r, :], w[r, :]) for r in tiles()]
    )
    extra = jnp.concatenate(
        [new_energy, new_curve, cross, jnp.zeros((EXTRA - 3, RHS), F32)], axis=0
    )
    restrict_into(groups, place, w, extra, bins, away, keep)


def stage2_kernel(
    groups, peers, counts, others, received, y, totals, cih, cil, high, low, scale, b,
    dots, before, u0, w0, m0, n0, u1, w1,
    p, s, u, w, last, scalars, m, n, coarse, pair,
):
    apply_all(
        groups, peers, counts, others, received, y, totals, cih, cil, high, low, scale,
        m, n, coarse, pair,
    )
    energy0, curve0, step0 = before[0:1, :], before[1:2, :], before[2:3, :]
    energy, delta, cross = dots[0:1, :], dots[1:2, :], dots[2:3, :]
    beta = energy / energy0
    curve = delta + beta * cross + beta * beta * curve0
    step = energy / curve
    scalars[...] = jnp.concatenate(
        [energy, curve, step, step0, jnp.zeros((EXTRA - 4, RHS), F32)], axis=0
    )
    for r in tiles():
        p[r, :] = u1[r, :] + beta * u0[r, :]
        s[r, :] = w1[r, :] + beta * w0[r, :]
        u[r, :] = u1[r, :] - step * (m[r, :] + beta * m0[r, :])
        w[r, :] = w1[r, :] - step * (n[r, :] + beta * n0[r, :])
    new_energy = column_dot(
        [((b[r, :] - step0 * w0[r, :]) - step * s[r, :], u[r, :]) for r in tiles()]
    )
    new_curve = column_dot([(w[r, :], u[r, :]) for r in tiles()])
    cross = column_dot(
        [(u[r, :], s[r, :]) for r in tiles()] + [(p[r, :], w[r, :]) for r in tiles()]
    )
    for slot in range(last.shape[0]):
        last[slot, 0:1, :] = new_energy
        last[slot, 1:2, :] = new_curve
        last[slot, 2:3, :] = cross


def finish_kernel(all_dots, scalars, b, u0, w0, p, s, u, w, solution, residual):
    value = jnp.sum(all_dots[...], axis=0)
    energy, delta, cross = value[0:1, :], value[1:2, :], value[2:3, :]
    before, curve0 = scalars[0:1, :], scalars[1:2, :]
    step1, step0 = scalars[2:3, :], scalars[3:4, :]
    beta = energy / before
    step = energy / (delta + beta * cross + beta * beta * curve0)
    along = step1 + step * beta
    for r in tiles():
        solution[r, :] = step0 * u0[r, :] + along * p[r, :] + step * u[r, :]
        residual[r, :] = (
            (b[r, :] - step0 * w0[r, :]) - along * s[r, :] - step * w[r, :]
        )


FIELD = ((DOF, RHS), F32)
MATRIX = ((DOF, DOF), BF16)
HALF_BINS = ((4, HEAD, RHS), F32)
SMALL = ((EXTRA, RHS), F32)
PAIR = pltpu.VMEM((DOF, 2 * RHS), BF16)
PAIRS = pltpu.VMEM((2, DOF, 2 * RHS), BF16)
FIELD_SCRATCH = pltpu.VMEM((DOF, RHS), F32)
BINS = pltpu.VMEM((NCB, HEAD, RHS), F32)
STEP_FLOPS = 2 * DOF * DOF * RHS * 3


def on_device(
    right_side,
    diagonal,
    stiffness,
    column_index,
    neighbours,
    face_count,
    corner_group,
    coarse_inverse,
):
    corners = lax.axis_size("corner")
    devices = corners * lax.axis_size("sub")
    b = right_side.reshape(DOF, RHS)
    place = lax.axis_index("corner").astype(jnp.int32).reshape(1)
    whole_inverse = lax.all_gather(coarse_inverse, "corner", axis=0, tiled=True)
    group_row = jnp.zeros((EXTRA, RHS), F32).at[0, :NCB].set(corner_group[0].astype(F32))
    scale = jnp.broadcast_to(diagonal.reshape(DOF, 1), (DOF, RHS))

    def exchange(array, bit):
        return lax.ppermute(array, "corner", [(i, i ^ bit) for i in range(corners)])

    def precondition(source, away, keep, extra):
        came1 = exchange(away, 1)
        x, h, e = call(
            chebyshev_first, "chebyshev_first", "vvvvv", "vvv", [FIELD] * 3, [PAIRS],
            STEP_FLOPS * SPLIT,
        )(source, scale, inverse, high, low)
        came2 = exchange(keep[2:] + came1[2:], 2)
        came3 = exchange(keep[1:2] + came1[1:2] + came2[1:2], 4)
        y, send = call(
            functools.partial(chebyshev_last, extra is not None), "chebyshev_last",
            "svvvvvvvvvvvv", "vv", [FIELD, ((NB, SLOT, RHS), F32)],
            [FIELD_SCRATCH, FIELD_SCRATCH, PAIRS], STEP_FLOPS * (DEGREE - 1 - SPLIT),
        )(
            neighbours, scale, inverse, high, low, x, h, e, keep, came1, came2, came3,
            group_row,
        )
        received = lax.all_to_all(send, "sub", 0, 0, tiled=True)
        total, dots = call(
            gather_kernel, "gather", "v", "vv", [((CHUNK, RHS), F32), SMALL]
        )(received)
        totals = lax.all_gather(total, "corner", axis=0, tiled=True)
        return received, y, totals, dots

    away, keep = call(
        restrict_kernel, "restrict", "ssv", "vv", [HALF_BINS] * 2, [BINS]
    )(corner_group, place, b)
    high, low, inverse = call(
        build_kernel, "build", "svv", "vvv", [MATRIX, MATRIX, FIELD],
        [pltpu.VMEM((DOF, DOF), F32)], STEP_FLOPS * 3,
    )(column_index, stiffness, scale)
    cih, cil = call(split_kernel, "split", "v", "vv", [MATRIX, MATRIX])(whole_inverse)

    received, y, totals, _ = precondition(b, away, keep, group_row)
    u0, w0, away, keep, others = call(
        stage0_kernel, "stage0", "ssssvvvvvvvvv", "vvvvs",
        [FIELD, FIELD, HALF_BINS, HALF_BINS, ((1, NCB), jnp.int32)],
        [FIELD_SCRATCH, PAIR, BINS], STEP_FLOPS * 2,
    )(
        corner_group, place, neighbours, face_count, received, y, totals, cih, cil,
        high, low, scale, b,
    )
    received, y, totals, dots = precondition(w0, away, keep, None)
    m0, n0, u1, w1, away, keep, before = call(
        stage1_kernel, "stage1", "sssssvvvvvvvvvvvv", "vvvvvvv",
        [FIELD] * 4 + [HALF_BINS, HALF_BINS, SMALL],
        [FIELD_SCRATCH, PAIR, BINS], STEP_FLOPS * 2,
    )(
        corner_group, place, neighbours, face_count, others, received, y, totals, cih, cil,
        high, low, scale, b, dots, u0, w0,
    )
    received, y, totals, dots = precondition(w1, away, keep, None)
    p, s, u2, w2, last, scalars = call(
        stage2_kernel, "stage2", "ssssvvvvvvvvvvvvvvvvv", "vvvvvv",
        [FIELD] * 4 + [((devices, 3, RHS), F32), SMALL],
        [FIELD_SCRATCH, FIELD_SCRATCH, FIELD_SCRATCH, PAIR], STEP_FLOPS * 2,
    )(
        corner_group, neighbours, face_count, others, received, y, totals, cih, cil,
        high, low, scale, b, dots, before, u0, w0, m0, n0, u1, w1,
    )
    all_dots = lax.all_to_all(last, ("sub", "corner"), 0, 0, tiled=True)
    solution, residual = call(
        finish_kernel, "finish", "vvvvvvvvv", "vv", [FIELD, FIELD]
    )(all_dots, scalars, b, u0, w0, p, s, u2, w2)
    return (solution.reshape(right_side.shape), residual.reshape(right_side.shape))


def solution(mesh):
    placed = (
        P(("sub", "corner"), None, None),
        P(("sub", "corner"), None),
        P(("sub", "corner"), None, None),
        P(("sub", "corner"), None),
        P(("sub", "corner"), None),
        P(("sub", "corner"), None),
        P(("sub", "corner"), None),
        P("corner", None),
    )
    return jax.shard_map(
        on_device,
        mesh=mesh,
        in_specs=placed,
        out_specs=(P(("sub", "corner"), None, None), P(("sub", "corner"), None, None)),
        check_vma=False,
    )
```

time: 1300 us -> 286 us (0.22)
  waiting for transfers between devices: 476 us -> 13.1 us
  matrix products: 210 us -> 0 us
  blocking collectives: 362 us -> 161 us
  local copies, waits for them, and re-layouts: 157 us -> 6.85 us
  Pallas kernels: 0 us -> 75.6 us
  other arithmetic: 62.6 us -> 0.09 us
    psum x5 -> x0, blocking collectives: 321 us -> none  [the longest x3 192 us: progress(): return lax.psum(column_dot(residual, corrected), ('sub', 'corner'))]
    psum x3 -> x0, waiting for transfers between devices: 307 us -> none  [coarse_term(): lax.psum(partial_sum.reshape(NG * block_width, load_count), ('sub', 'corn...]
    dot_general x57 -> x0, matrix products: 210 us -> none  [the longest x24 102 us: local_product(): jnp.einsum('bij,bjr->bir', stiffness, picked, precision=HIGHEST_PRECISION)]
    all_gather x3 -> x1, waiting for transfers between devices: 169 us -> 0.01 us  [on_device(): whole_inverse = lax.all_gather(coarse_inverse, 'corner', axis=0, tiled=True)]
    gather x51 -> x0, local copies, waits for them, and re-layouts: 144 us -> none  [the longest x24 78.5 us: local_product(): spread = jnp.sum(backward[inverse_index, link_index[None, :]], axis=1)]
    all_to_all x0 -> x4, blocking collectives: none -> 114 us  [the longest x3 99.1 us: precondition(): received = lax.all_to_all(send, 'sub', 0, 0, tiled=True)]
    pallas_call x0 -> x16, Pallas kernels: none -> 75.6 us  [the longest x3 21 us: precondition(): call(functools.partial(chebyshev_last, extra is not None), 'chebyshev_las...]
    reduce_sum x26 -> x0, other arithmetic: 50.7 us -> none  [the longest x24 50.4 us: local_product(): spread = jnp.sum(backward[inverse_index, link_index[None, :]], axis=1)]
  transfers between devices with their start and end apart: 6 -> 10, of which waited for: 6 -> 4; matrix products, arithmetic and copies ran while one was open for 12% -> 1% of each run, Pallas kernels for 0% -> 13%
where the time goes in v1:
time: 286 us; the launch traced here: 281 us
  blocking collectives  161 us (56%)
  Pallas kernels  75.6 us (26%)
  between operations  14.5 us (5%)
  waiting for transfers between devices  13.1 us (5%)
  starting transfers between devices  9.89 us (3%)
  local copies, waits for them, and re-layouts  6.85 us (2%)
    all_to_all x3, blocking collectives, precondition(): received = lax.all_to_all(send, 'sub', 0, 0, tiled=True)  99.1 us
    all_gather x3, blocking collectives, precondition(): totals = lax.all_gather(total, 'corner', axis=0, tiled=True)  47.2 us
    pallas_call x3, Pallas kernels, precondition(): call(functools.partial(chebyshev_last, extra is not None), 'chebyshev_las...  21 us
    pallas_call x3, Pallas kernels, precondition(): call(chebyshev_first, 'chebyshev_first', 'vvvvv', 'vvv', [FIELD] * 3, [PA...  20.5 us
    all_to_all x1, blocking collectives, on_device(): all_dots = lax.all_to_all(last, ('sub', 'corner'), 0, 0, tiled=True)  14.8 us
    ppermute x9, waiting for transfers between devices, exchange(): return lax.ppermute(array, 'corner', [(i, i ^ bit) for i in range(corners)])  12.5 us
    ppermute x9, starting transfers between devices, exchange(): return lax.ppermute(array, 'corner', [(i, i ^ bit) for i in range(corners)])  9.85 us
    pallas_call x1, Pallas kernels, on_device(): call(stage0_kernel, 'stage0', 'ssssvvvvvvvvv', 'vvvvs', [FIELD, FIELD, HA...  7.41 us
  transfers between devices with their start and end apart: 10, of which 4 were waited for; matrix products, arithmetic and copies ran while one was open for 1% of the time, Pallas kernels for 13%

profile of v1, /device:TPU:1, one launch (start us, length us, event | category | flops | bytes accessed | tf_op | source)
XLA Modules:
  0.0 281.2 jit_solution(6907907609744236346)
XLA Ops:
  7.2 0.0 all-gather.2.cloned.1.call-start
  7.2 0.7 all-gather.2.cloned.1.call-update
  7.9 1.0 copy-done.8
  8.9 0.7 copy-done.16
  9.6 0.7 restrict.1
  10.3 1.5 collective-permute-start
  11.8 0.8 broadcast_in_dim.8
  12.5 0.8 copy.10.column
  13.3 1.4 collective-permute-start.1
  14.7 0.2 broadcast_in_dim.9.scale
  14.9 0.0 copy-start.20
  14.9 1.2 copy-done.20
  16.1 6.4 %build.1 = (bf16[1024,1024]{1,0:T(8,128)(2,1)S(1)}, bf16[1024,1024]{1,0:T(8,128)(2,1)}, f32[1024,128]{1,0:T(8,128)S(1)}) custom-call(s32[16,3]{1,0:T(8,128)S(1)} %copy.10.column, f32[16,64,192]{2,1,0:T(8,128)S(1)} %copy-done.20, f32[1024,128]{1,0:T(8,128)S(1)} %broadcast_in_dim.9.scale), custom_call_target="tpu_custom_call" | custom-call | flops 2415919104 | bytes 4194304 | tf_op jit(solution)/shard_map/build/pallas_call | solution.py:376
  22.5 2.7 collective-permute-start.2
  25.3 6.9 %chebyshev_first.3 = (f32[1024,128]{1,0:T(8,128)S(1)}, f32[1024,128]{1,0:T(8,128)S(1)}, f32[1024,128]{1,0:T(8,128)S(1)}) custom-call(f32[1024,128]{1,0:T(8,128)S(1)} %bitcast.5, f32[1024,128]{1,0:T(8,128)S(1)} %broadcast_in_dim.9.scale, f32[1024,128]{1,0:T(8,128)S(1)} %get-tuple-element.61.inverse, bf16[1024,1024]{1,0:T(8,128)(2,1)S(1)} %get-tuple-element.62.high, ...), custom_call_target="tpu_custom_call" | custom-call | flops 3221225472 | bytes 4194304 | tf_op jit(solution)/shard_map/chebyshev_first/pallas_call | solution.py:352
  32.2 7.1 %chebyshev_last.3 = (f32[1024,128]{1,0:T(8,128)S(1)}, f32[16,264,128]{2,1,0:T(8,128)}) custom-call(s32[1,8]{1,0:T(1,128)S(1)} %copy-done.18, f32[1024,128]{1,0:T(8,128)S(1)} %broadcast_in_dim.9.scale, f32[1024,128]{1,0:T(8,128)S(1)} %get-tuple-element.61.inverse, bf16[1024,1024]{1,0:T(8,128)(2,1)S(1)} %get-tuple-element.62.high, ...), custom_call_target="tpu_custom_call" | custom-call | flops 2415919104 | bytes 4194304 | tf_op jit(solution)/shard_map/chebyshev_last/pallas_call | solution.py:358
  39.3 36.1 %all_to_all.20.received = f32[16,264,128]{2,1,0:T(8,128)S(1)} all-to-all(f32[16,264,128]{2,1,0:T(8,128)} %get-tuple-element.69), channel_id=1, replica_groups=mesh['sub'=16,'corner'=8] {'sub'}, dimensions={0} | all-to-all | bytes 4325376 | tf_op jit(solution)/shard_map/all_to_all | solution.py:366
  75.4 0.7 gather.3
  76.2 16.2 %all_gather.12.totals = f32[1024,128]{1,0:T(8,128)} all-gather(f32[128,128]{1,0:T(8,128)S(1)} %get-tuple-element.71), channel_id=1, replica_groups=mesh['sub'=16,'corner'=8] {'corner'}, dimensions={0}, use_global_device_ids=true | all-gather | bytes 589824 | tf_op jit(solution)/shard_map/all_gather | solution.py:370
  92.3 2.8 %split.1 = (bf16[1024,1024]{1,0:T(8,128)(2,1)S(1)}, bf16[1024,1024]{1,0:T(8,128)(2,1)S(1)}) custom-call(f32[1024,1024]{1,0:T(8,128)} %all-gather.2.cloned.1.call-done.value), custom_call_target="tpu_custom_call" | custom-call | bytes 4194304 | tf_op jit(solution)/shard_map/split/pallas_call | solution.py:380
  95.2 1.4 copy-done.7
  96.6 0.0 copy-start.22
  96.6 7.4 %stage0.1 = (f32[1024,128]{1,0:T(8,128)S(1)}, f32[1024,128]{1,0:T(8,128)S(1)}, f32[4,136,128]{2,1,0:T(8,128)S(1)}, f32[4,136,128]{2,1,0:T(8,128)S(1)}, s32[1,8]{1,0:T(1,128)S(1)}) custom-call(s32[1,8]{1,0:T(1,128)S(1)} %copy-done.17, s32[1]{0:T(128)} %bitcast.place, s32[1,8]{1,0:T(1,128)S(1)} %copy-done.18, s32[1,8]{1,0:T(1,128)S(1)} %copy-done.19, ...), custom_call_target="tpu_custom_call" | custom-call | flops 1610612736 | bytes 4194304 | tf_op jit(solution)/shard_map/stage0/pallas_call | solution.py:383
  104.0 0.3 collective-permute-start.3
  104.3 1.4 collective-permute-done.3.came1
  105.7 0.1 collective-permute-start.4
  105.8 5.1 %collective-permute-done.4.came2 = f32[2,136,128]{2,1,0:T(8,128)S(1)} collective-permute-done((f32[2,136,128]{2,1,0:T(8,128)S(1)}, f32[2,136,128]{2,1,0:T(8,128)S(1)}, u32[]{:S(2)}, u32[]{:S(2)}) %collective-permute-start.4) | collective-permute-done | bytes 139296 | tf_op jit(solution)/shard_map/ppermute | solution.py:348
  110.9 1.3 collective-permute-start.5
  112.2 6.7 %chebyshev_first.4 = (f32[1024,128]{1,0:T(8,128)S(1)}, f32[1024,128]{1,0:T(8,128)S(1)}, f32[1024,128]{1,0:T(8,128)S(1)}) custom-call(f32[1024,128]{1,0:T(8,128)S(1)} %get-tuple-element.75.source.w0, f32[1024,128]{1,0:T(8,128)S(1)} %broadcast_in_dim.9.scale, f32[1024,128]{1,0:T(8,128)S(1)} %copy-done.22, bf16[1024,1024]{1,0:T(8,128)(2,1)S(1)} %copy-done.4, ...), custom_call_target="tpu_custom_call" | custom-call | flops 3221225472 | bytes 4194304 | tf_op jit(solution)/shard_map/chebyshev_first/pallas_call | solution.py:352
  118.9 6.9 %chebyshev_last.4 = (f32[1024,128]{1,0:T(8,128)S(1)}, f32[16,264,128]{2,1,0:T(8,128)}) custom-call(s32[1,8]{1,0:T(1,128)S(1)} %copy-done.18, f32[1024,128]{1,0:T(8,128)S(1)} %broadcast_in_dim.9.scale, f32[1024,128]{1,0:T(8,128)S(1)} %copy-done.22, bf16[1024,1024]{1,0:T(8,128)(2,1)S(1)} %copy-done.4, bf16[1024,1024]{1,0:T(8,128)(2,1)} %get-tuple-element.63.low, ...), custom_call_target="tpu_custom_call" | custom-call | flops 2415919104 | bytes 4194304 | tf_op jit(solution)/shard_map/chebyshev_last/pallas_call | solution.py:358
  125.9 31.1 %all_to_all.21.received = f32[16,264,128]{2,1,0:T(8,128)S(1)} all-to-all(f32[16,264,128]{2,1,0:T(8,128)} %get-tuple-element.81), channel_id=1, replica_groups=mesh['sub'=16,'corner'=8] {'sub'}, dimensions={0} | all-to-all | bytes 4325376 | tf_op jit(solution)/shard_map/all_to_all | solution.py:366
  157.0 0.1 gather.4
  157.0 15.9 %all_gather.14.totals = f32[1024,128]{1,0:T(8,128)S(1)} all-gather(f32[128,128]{1,0:T(8,128)S(1)} %get-tuple-element.83), channel_id=1, replica_groups=mesh['sub'=16,'corner'=8] {'corner'}, dimensions={0}, use_global_device_ids=true | all-gather | bytes 589824 | tf_op jit(solution)/shard_map/all_gather | solution.py:370
  173.0 7.1 %stage1.1 = (f32[1024,128]{1,0:T(8,128)S(1)}, f32[1024,128]{1,0:T(8,128)S(1)}, f32[1024,128]{1,0:T(8,128)S(1)}, f32[1024,128]{1,0:T(8,128)S(1)}, f32[4,136,128]{...) custom-call(s32[1,8]{1,0:T(1,128)S(1)} %copy-done.17, s32[1]{0:T(128)} %bitcast.place, ...), custom_call_target="tpu_custom_call" | custom-call | flops 1610612736 | bytes 4194304 | tf_op jit(solution)/shard_map/stage1/pallas_call | solution.py:392
  180.1 0.8 copy-done.14
  180.9 0.2 collective-permute-start.6
  181.0 1.4 collective-permute-done.6.came1
  182.4 0.6 collective-permute-start.7
  183.1 4.6 %collective-permute-done.7.came2 = f32[2,136,128]{2,1,0:T(8,128)S(1)} collective-permute-done((f32[2,136,128]{2,1,0:T(8,128)S(1)}, f32[2,136,128]{2,1,0:T(8,128)S(1)}, u32[]{:S(2)}, u32[]{:S(2)}) %collective-permute-start.7) | collective-permute-done | bytes 139296 | tf_op jit(solution)/shard_map/ppermute | solution.py:348
  187.7 1.9 collective-permute-start.8
  189.5 6.9 %chebyshev_first.5 = (f32[1024,128]{1,0:T(8,128)S(1)}, f32[1024,128]{1,0:T(8,128)S(1)}, f32[1024,128]{1,0:T(8,128)S(1)}) custom-call(f32[1024,128]{1,0:T(8,128)S(1)} %get-tuple-element.86.source.w1, f32[1024,128]{1,0:T(8,128)S(1)} %broadcast_in_dim.9.scale, f32[1024,128]{1,0:T(8,128)S(1)} %copy-done.22, bf16[1024,1024]{1,0:T(8,128)(2,1)S(1)} %copy-done.5, ...), custom_call_target="tpu_custom_call" | custom-call | flops 3221225472 | bytes 4194304 | tf_op jit(solution)/shard_map/chebyshev_first/pallas_call | solution.py:352
  196.4 7.0 %chebyshev_last.5 = (f32[1024,128]{1,0:T(8,128)S(1)}, f32[16,264,128]{2,1,0:T(8,128)}) custom-call(s32[1,8]{1,0:T(1,128)S(1)} %copy-done.18, f32[1024,128]{1,0:T(8,128)S(1)} %broadcast_in_dim.9.scale, f32[1024,128]{1,0:T(8,128)S(1)} %copy-done.22, bf16[1024,1024]{1,0:T(8,128)(2,1)S(1)} %copy-done.5, bf16[1024,1024]{1,0:T(8,128)(2,1)} %get-tuple-element.63.low, ...), custom_call_target="tpu_custom_call" | custom-call | flops 2415919104 | bytes 4194304 | tf_op jit(solution)/shard_map/chebyshev_last/pallas_call | solution.py:358
  203.5 31.9 %all_to_all.22.received = f32[16,264,128]{2,1,0:T(8,128)S(1)} all-to-all(f32[16,264,128]{2,1,0:T(8,128)} %get-tuple-element.92), channel_id=1, replica_groups=mesh['sub'=16,'corner'=8] {'sub'}, dimensions={0} | all-to-all | bytes 4325376 | tf_op jit(solution)/shard_map/all_to_all | solution.py:366
  235.3 0.1 gather.5
  235.4 15.2 %all_gather.15.totals = f32[1024,128]{1,0:T(8,128)S(1)} all-gather(f32[128,128]{1,0:T(8,128)S(1)} %get-tuple-element.94), channel_id=1, replica_groups=mesh['sub'=16,'corner'=8] {'corner'}, dimensions={0}, use_global_device_ids=true | all-gather | bytes 589824 | tf_op jit(solution)/shard_map/all_gather | solution.py:370
  250.6 7.4 %stage2.1 = (f32[1024,128]{1,0:T(8,128)S(1)}, f32[1024,128]{1,0:T(8,128)S(1)}, f32[1024,128]{1,0:T(8,128)S(1)}, f32[1024,128]{1,0:T(8,128)S(1)}, f32[128,3,128]{2,1,0:T(4,128)S(1)}, /*index=5*/f32[8,128]{1,0:T(8,128)S(1)}) custom-call(s32[1,8]{1,0:T(1,128)S(1)} %copy-done.17, s32[1,8]{1,0:T(1,128)S(1)} %copy-done.18, s32[1,8]{1,0:T(1,128)S(1)} %copy-done.19, ...), custom_call_target="tpu_custom_call" | custom-call | flops 1610612736 | bytes 4194304 | tf_op jit(solution)/shard_map/stage2/pallas_call | solution.py:401
  258.0 14.8 %all_to_all.23.all_dots = f32[128,3,128]{2,1,0:T(4,128)S(1)} all-to-all(f32[128,3,128]{2,1,0:T(4,128)S(1)} %get-tuple-element.100), channel_id=1, replica_groups=mesh['sub'=16,'corner'=8] {'sub','corner'}, dimensions={0} | all-to-all | bytes 393216 | tf_op jit(solution)/shard_map/all_to_all | solution.py:409
  272.8 1.4 finish.1
  (53 shorter events, 0.2 us)
Async XLA Ops:
  7.2 85.2 %all-gather.2.cloned.1.call-start = ((), (), s32[]{:S(2)}) async-start(), calls=%async_computation.4 | async-start | bytes 4718592 | tf_op jit(solution)/shard_map/all_gather | solution.py:343
  7.9 1.0 copy-start.8
  8.9 0.7 copy-start.16
  10.3 3.0 %collective-permute-start = (f32[4,136,128]{2,1,0:T(8,128)S(1)}, f32[4,136,128]{2,1,0:T(8,128)S(1)}, u32[]{:S(2)}, u32[]{:S(2)}) collective-permute-start(f32[4,136,128]{2,1,0:T(8,128)S(1)} %get-tuple-element.68), channel_id=1, source_target_pairs={{0,1},{1,0},{2,3},{3,2},{4,5},{5,4},{6,7},{7,6},{8,9},{9,8},{10,11... | collective-permute-start | bytes 835592 | tf_op jit(solution)/shard_map/ppermute | solution.py:348
  13.3 9.2 %collective-permute-start.1 = (f32[2,136,128]{2,1,0:T(8,128)S(1)}, f32[2,136,128]{2,1,0:T(8,128)S(1)}, u32[]{:S(2)}, u32[]{:S(2)}) collective-permute-start(f32[2,136,128]{2,1,0:T(8,128)S(1)} %slice_add_fusion.2), channel_id=1, source_target_pairs={{0,2},{1,3},{2,0},{3,1},{4,6},{5,7},{6,4},{7,5},{8,10},{9,11},{10,... | collective-permute-start | bytes 417800 | tf_op jit(solution)/shard_map/ppermute | solution.py:348
  14.9 1.2 copy-start.20
  16.1 9.1 %copy-start.9 = (f32[16,64,128]{2,1,0:T(8,128)S(1)}, f32[16,64,128]{2,1,0:T(8,128)}, u32[]{:S(2)}) copy-start(f32[16,64,128]{2,1,0:T(8,128)} %param.10) | copy-start | bytes 1572868
  22.5 9.7 %copy-start.3 = (bf16[1024,1024]{1,0:T(8,128)(2,1)}, bf16[1024,1024]{1,0:T(8,128)(2,1)S(1)}, u32[]{:S(2)}) copy-start(bf16[1024,1024]{1,0:T(8,128)(2,1)S(1)} %get-tuple-element.62.high) | copy-start | bytes 6291460
  22.5 9.7 %copy-start.21 = (f32[1024,128]{1,0:T(8,128)}, f32[1024,128]{1,0:T(8,128)S(1)}, u32[]{:S(2)}) copy-start(f32[1024,128]{1,0:T(8,128)S(1)} %get-tuple-element.61.inverse) | copy-start | bytes 1572868
  22.5 9.7 %collective-permute-start.2 = (f32[1,136,128]{2,1,0:T(8,128)S(1)}, f32[1,136,128]{2,1,0:T(8,128)S(1)}, u32[]{:S(2)}, u32[]{:S(2)}) collective-permute-start(f32[1,136,128]{2,1,0:T(8,128)S(1)} %slice_add_fusion.7), channel_id=1, source_target_pairs={{0,4},{1,5},{2,6},{3,7},{4,0},{5,1},{6,2},{7,3},{8,12},{9,13},{10,... | collective-permute-start | bytes 208904 | tf_op jit(solution)/shard_map/ppermute | solution.py:348
  25.2 6.9 %copy-start.17 = (s32[1,8]{1,0:T(1,128)S(1)}, s32[1,8]{1,0:T(1,128)}, u32[]{:S(2)}) copy-start(s32[1,8]{1,0:T(1,128)} %groups.7) | copy-start | bytes 100
  25.2 7.0 %copy-start.18 = (s32[1,8]{1,0:T(1,128)S(1)}, s32[1,8]{1,0:T(1,128)}, u32[]{:S(2)}) copy-start(s32[1,8]{1,0:T(1,128)} %peers.11) | copy-start | bytes 100
  39.3 36.1 %copy-start.11 = (f32[1024,128]{1,0:T(8,128)}, f32[1024,128]{1,0:T(8,128)S(1)}, u32[]{:S(2)}) copy-start(f32[1024,128]{1,0:T(8,128)S(1)} %get-tuple-element.70.y) | copy-start | bytes 1572868
  75.4 19.7 %copy-start = (f32[16,264,128]{2,1,0:T(8,128)}, f32[16,264,128]{2,1,0:T(8,128)S(1)}, u32[]{:S(2)}) copy-start(f32[16,264,128]{2,1,0:T(8,128)S(1)} %all_to_all.20.received) | copy-start | bytes 6488068
  92.3 4.2 %copy-start.19 = (s32[1,8]{1,0:T(1,128)S(1)}, s32[1,8]{1,0:T(1,128)}, u32[]{:S(2)}) copy-start(s32[1,8]{1,0:T(1,128)} %counts.5) | copy-start | bytes 100
  92.3 4.2 %copy-start.10 = (f32[1024,128]{1,0:T(8,128)S(1)}, f32[1024,128]{1,0:T(8,128)}, u32[]{:S(2)}) copy-start(f32[1024,128]{1,0:T(8,128)} %all_gather.12.totals) | copy-start | bytes 1572868
  92.3 4.2 %copy-start.12 = (f32[1024,128]{1,0:T(8,128)S(1)}, f32[1024,128]{1,0:T(8,128)}, u32[]{:S(2)}) copy-start(f32[1024,128]{1,0:T(8,128)} %copy-done.11) | copy-start | bytes 1572868
  95.2 1.4 copy-start.7
  96.6 7.5 %copy-start.6 = (bf16[1024,1024]{1,0:T(8,128)(2,1)}, bf16[1024,1024]{1,0:T(8,128)(2,1)S(1)}, u32[]{:S(2)}) copy-start(bf16[1024,1024]{1,0:T(8,128)(2,1)S(1)} %get-tuple-element.72.cih) | copy-start | bytes 6291460
  96.6 15.6 %copy-start.4 = (bf16[1024,1024]{1,0:T(8,128)(2,1)S(1)}, bf16[1024,1024]{1,0:T(8,128)(2,1)}, u32[]{:S(2)}) copy-start(bf16[1024,1024]{1,0:T(8,128)(2,1)} %copy-done.3) | copy-start | bytes 6291460
  96.6 15.6 %copy-start.22 = (f32[1024,128]{1,0:T(8,128)S(1)}, f32[1024,128]{1,0:T(8,128)}, u32[]{:S(2)}) copy-start(f32[1024,128]{1,0:T(8,128)} %copy-done.21) | copy-start | bytes 1572868
  104.0 1.6 collective-permute-start.3
  105.7 5.2 %collective-permute-start.4 = (f32[2,136,128]{2,1,0:T(8,128)S(1)}, f32[2,136,128]{2,1,0:T(8,128)S(1)}, u32[]{:S(2)}, u32[]{:S(2)}) collective-permute-start(f32[2,136,128]{2,1,0:T(8,128)S(1)} %slice_add_fusion.1), channel_id=1, source_target_pairs={{0,2},{1,3},{2,0},{3,1},{4,6},{5,7},{6,4},{7,5},{8,10},{9,11},{10,... | collective-permute-start | bytes 417800 | tf_op jit(solution)/shard_map/ppermute | solution.py:348
  110.9 8.0 %collective-permute-start.5 = (f32[1,136,128]{2,1,0:T(8,128)S(1)}, f32[1,136,128]{2,1,0:T(8,128)S(1)}, u32[]{:S(2)}, u32[]{:S(2)}) collective-permute-start(f32[1,136,128]{2,1,0:T(8,128)S(1)} %slice_add_fusion.5), channel_id=1, source_target_pairs={{0,4},{1,5},{2,6},{3,7},{4,0},{5,1},{6,2},{7,3},{8,12},{9,13},{10,... | collective-permute-start | bytes 208904 | tf_op jit(solution)/shard_map/ppermute | solution.py:348
  157.0 16.0 %copy-start.1 = (f32[16,264,128]{2,1,0:T(8,128)}, f32[16,264,128]{2,1,0:T(8,128)S(1)}, u32[]{:S(2)}) copy-start(f32[16,264,128]{2,1,0:T(8,128)S(1)} %all_to_all.21.received) | copy-start | bytes 6488068
  172.9 16.6 %copy-start.5 = (bf16[1024,1024]{1,0:T(8,128)(2,1)S(1)}, bf16[1024,1024]{1,0:T(8,128)(2,1)}, u32[]{:S(2)}) copy-start(bf16[1024,1024]{1,0:T(8,128)(2,1)} %copy-done.3) | copy-start | bytes 6291460
  180.1 0.8 copy-start.14
  180.9 15.6 %copy-start.13 = (f32[1024,128]{1,0:T(8,128)}, f32[1024,128]{1,0:T(8,128)S(1)}, u32[]{:S(2)}) copy-start(f32[1024,128]{1,0:T(8,128)S(1)} %get-tuple-element.98.n0) | copy-start | bytes 1572868
  180.9 15.6 %copy-start.15 = (f32[1024,128]{1,0:T(8,128)}, f32[1024,128]{1,0:T(8,128)S(1)}, u32[]{:S(2)}) copy-start(f32[1024,128]{1,0:T(8,128)S(1)} %get-tuple-element.86.source.w1) | copy-start | bytes 1572868
  180.9 1.6 collective-permute-start.6
  182.4 5.2 %collective-permute-start.7 = (f32[2,136,128]{2,1,0:T(8,128)S(1)}, f32[2,136,128]{2,1,0:T(8,128)S(1)}, u32[]{:S(2)}, u32[]{:S(2)}) collective-permute-start(f32[2,136,128]{2,1,0:T(8,128)S(1)} %slice_add_fusion), channel_id=1, source_target_pairs={{0,2},{1,3},{2,0},{3,1},{4,6},{5,7},{6,4},{7,5},{8,10},{9,11},{10,... | collective-permute-start | bytes 417800 | tf_op jit(solution)/shard_map/ppermute | solution.py:348
  187.7 8.8 %collective-permute-start.8 = (f32[1,136,128]{2,1,0:T(8,128)S(1)}, f32[1,136,128]{2,1,0:T(8,128)S(1)}, u32[]{:S(2)}, u32[]{:S(2)}) collective-permute-start(f32[1,136,128]{2,1,0:T(8,128)S(1)} %slice_add_fusion.3), channel_id=1, source_target_pairs={{0,4},{1,5},{2,6},{3,7},{4,0},{5,1},{6,2},{7,3},{8,12},{9,13},{10,... | collective-permute-start | bytes 208904 | tf_op jit(solution)/shard_map/ppermute | solution.py:348
  235.3 15.2 %copy-start.2 = (f32[16,264,128]{2,1,0:T(8,128)}, f32[16,264,128]{2,1,0:T(8,128)S(1)}, u32[]{:S(2)}) copy-start(f32[16,264,128]{2,1,0:T(8,128)S(1)} %all_to_all.22.received) | copy-start | bytes 6488068
Sparse Core Ops, SparseCore 0:
  9.7 37.1 all-gather.1

commit v2 on v1

--- a/solution.py
+++ b/solution.py
@@ -1,4 +1,5 @@
 import functools
+import math
 
 import jax
 import jax.numpy as jnp
@@ -21,31 +22,46 @@
 HALF_RANGE = 0.8
 SIGMA = 1.0 / HALF_RANGE
 CHUNK = 128
+PIECE = 8
 EXTRA = 8
-HEAD = CHUNK + EXTRA
+HEAD = PIECE + EXTRA
 SLOT = HEAD + 2 * BLOCK
 TILE = 256
-SPLIT = 4
-VMEM_LIMIT = 48 * 1024 * 1024
+CUTS = (0, 1, 6)
+VMEM_ROOM = 3 * 1024 * 1024
 
 
 def spec(kind):
     return pl.BlockSpec(memory_space=pltpu.SMEM if kind == "s" else pltpu.VMEM)
 
 
+def nbytes(shape, dtype):
+    lanes = -(-shape[-1] // 128) * 128
+    rows = -(-shape[-2] // 8) * 8
+    return math.prod(shape[:-2]) * rows * lanes * jnp.dtype(dtype).itemsize
+
+
 def call(body, name, kinds, out_kinds, outs, scratch=(), flops=0):
-    return pl.pallas_call(
-        body,
-        name=name,
-        in_specs=[spec(k) for k in kinds],
-        out_specs=tuple(spec(k) for k in out_kinds),
-        out_shape=tuple(jax.ShapeDtypeStruct(s, t) for s, t in outs),
-        scratch_shapes=list(scratch),
-        compiler_params=pltpu.CompilerParams(vmem_limit_bytes=VMEM_LIMIT),
-        cost_estimate=pl.CostEstimate(
-            flops=flops, bytes_accessed=4 * 1024 * 1024, transcendentals=0
-        ),
-    )
+    def run(*operands):
+        vmem = [(a.shape, a.dtype) for a, k in zip(operands, kinds, strict=True) if k == "v"]
+        vmem += [o for o, k in zip(outs, out_kinds, strict=True) if k == "v"]
+        vmem += [(s.shape, s.dtype) for s in scratch]
+        return pl.pallas_call(
+            body,
+            name=name,
+            in_specs=[spec(k) for k in kinds],
+            out_specs=tuple(spec(k) for k in out_kinds),
+            out_shape=tuple(jax.ShapeDtypeStruct(s, t) for s, t in outs),
+            scratch_shapes=list(scratch),
+            compiler_params=pltpu.CompilerParams(
+                vmem_limit_bytes=VMEM_ROOM + sum(nbytes(*v) for v in vmem)
+            ),
+            cost_estimate=pl.CostEstimate(
+                flops=flops, bytes_accessed=4 * 1024 * 1024, transcendentals=0
+            ),
+        )(*operands)
+
+    return run
 
 
 def tiles():
@@ -64,26 +80,44 @@
     return both[:, :RHS] + (both[:, RHS:] + rest)
 
 
-def build_kernel(column, stiffness, scale, high, low, inverse, total):
-    total[...] = jnp.zeros_like(total)
+def build_kernel(
+    column, groups, place, stiffness, scale, b,
+    high, low, inverse, away, keep, turned, even, odd, source, bins,
+):
+    restrict_into(groups, place, b, None, bins, away, keep)
     lane_half = lax.broadcasted_iota(jnp.int32, (BLOCK, 2 * BLOCK), 1) // BLOCK
+    for pair in range(NB // 2):
+        tile = stiffness[2 * pair : 2 * pair + 2]
+        first = tile[:, :, : 2 * BLOCK].reshape(2 * BLOCK, 2 * BLOCK).T
+        turned[pair, 0] = first[:BLOCK]
+        turned[pair, 1] = first[BLOCK:]
+        turned[pair, 2] = tile[:, :, 2 * BLOCK :].reshape(2 * BLOCK, BLOCK).T
     for row in range(NB):
         for link in range(BW):
-            part = stiffness[row, :, link * BLOCK : (link + 1) * BLOCK]
-            turned = part.T
-            target = column[row, link]
-            offset = pl.multiple_of((target // 2) * 2 * BLOCK, 2 * BLOCK)
-            rows = slice(row * BLOCK, (row + 1) * BLOCK)
-            total[rows, pl.ds(offset, 2 * BLOCK)] += jnp.where(
-                lane_half == target % 2, jnp.concatenate([part, part], axis=1), 0.0
-            )
-            lanes = slice((row // 2) * 2 * BLOCK, (row // 2 + 1) * 2 * BLOCK)
-            below = pl.ds(pl.multiple_of(target * BLOCK, BLOCK), BLOCK)
-            total[below, lanes] += jnp.where(
-                lane_half == row % 2, jnp.concatenate([turned, turned], axis=1), 0.0
-            )
-    for rows in tiles():
-        value = total[rows, :]
+            source[column[row, link], link] = row
+    for row in range(NB):
+        panel = odd if row % 2 else even
+        panel[...] = jnp.zeros_like(panel)
+        tile = stiffness[row, :, : 2 * BLOCK]
+        swapped = pltpu.roll(tile, BLOCK, 1)
+        last = stiffness[row, :, 2 * BLOCK :]
+        twice = (
+            jnp.where(lane_half == 0, tile, swapped),
+            jnp.where(lane_half == 1, tile, swapped),
+            jnp.concatenate([last, last], axis=1),
+        )
+        for link in range(BW):
+            origin = source[row, link]
+            for column_block, block in (
+                (column[row, link], twice[link]),
+                (origin, turned[origin // 2, link]),
+            ):
+                lanes = pl.ds(
+                    pl.multiple_of((column_block // 2) * 2 * BLOCK, 2 * BLOCK), 2 * BLOCK
+                )
+                panel[:, lanes] += jnp.where(lane_half == column_block % 2, block, 0.0)
+        rows = slice(row * BLOCK, (row + 1) * BLOCK)
+        value = panel[...]
         top = value.astype(BF16)
         high[rows, :] = top
         low[rows, :] = (value - top.astype(F32)).astype(BF16)
@@ -112,10 +146,6 @@
             bins[slot, CHUNK:, :] = extra
     keep[...] = bins[:4]
     away[...] = bins[4:]
-
-
-def restrict_kernel(groups, place, vector, away, keep, bins):
-    restrict_into(groups, place, vector, None, bins, away, keep)
 
 
 def chebyshev_steps(first, last, scale, inverse, high, low, x, h, e, pairs):
@@ -138,43 +168,60 @@
         ratio = later
 
 
-def chebyshev_first(source, scale, inverse, high, low, x, h, e, pairs):
+def chebyshev_first(last, source, scale, inverse, high, low, x, h, e, pairs):
     for rows in tiles():
         value = source[rows, :]
         h[rows, :] = value
         value = value * inverse[rows, :]
         e[rows, :] = value
         put_split(pairs.at[0], rows, value)
-    chebyshev_steps(0, SPLIT, scale, inverse, high, low, x, h, e, pairs)
+    chebyshev_steps(0, last, scale, inverse, high, low, x, h, e, pairs)
+
+
+def resume(first, x0, h0, e0, x, h, e, pairs):
+    for rows in tiles():
+        x[rows, :] = x0[rows, :]
+        h[rows, :] = h0[rows, :]
+        value = e0[rows, :]
+        e[rows, :] = value
+        put_split(pairs.at[first % 2], rows, value)
+
+
+def chebyshev_middle(first, last, x0, h0, e0, scale, inverse, high, low, x, h, e, pairs):
+    resume(first, x0, h0, e0, x, h, e, pairs)
+    chebyshev_steps(first, last, scale, inverse, high, low, x, h, e, pairs)
 
 
 def chebyshev_last(
-    with_groups, peers, scale, inverse, high, low, x0, h0, e0, kept, came1, came2, came3, extra,
-    y, send, h, e, pairs,
-):
-    y[...] = x0[...]
-    h[...] = h0[...]
-    e[...] = e0[...]
-    for rows in tiles():
-        put_split(pairs.at[SPLIT % 2], rows, e0[rows, :])
-    chebyshev_steps(SPLIT, DEGREE - 1, scale, inverse, high, low, y, h, e, pairs)
+    with_groups, first, peers, groups, scale, inverse, high, low, x0, h0, e0, kept, came1,
+    came2, came3, came4, y, send, h, e, pairs,
+):
+    resume(first, x0, h0, e0, y, h, e, pairs)
+    chebyshev_steps(first, DEGREE - 1, scale, inverse, high, low, y, h, e, pairs)
     y[...] += e[...]
-    head = kept[0] + came1[0] + (came2[0] + came3[0])
+    head = kept[0] + came1[0] + (came2[0] + came3[0] + came4[0])
+    tail = head[CHUNK:, :]
+    if with_groups:
+        lanes = lax.broadcasted_iota(jnp.int32, (EXTRA, RHS), 1)
+        tail = jnp.zeros((EXTRA, RHS), F32)
+        for corner in range(NCB):
+            group = groups[0, corner].astype(F32)
+            tail = jnp.where(lanes == corner, group, tail)
     for slot in range(NB):
-        send[slot, :HEAD, :] = head
-        if with_groups:
-            send[slot, CHUNK:HEAD, :] = extra[...]
+        send[slot, :PIECE, :] = head[slot * PIECE : (slot + 1) * PIECE, :]
+        send[slot, PIECE:HEAD, :] = tail
         send[slot, HEAD:, :] = jnp.zeros((2 * BLOCK, RHS), F32)
     for turn in range(ROUNDS):
         send[peers[0, turn], HEAD:, :] = y[turn * 2 * BLOCK : (turn + 1) * 2 * BLOCK, :]
 
 
-def gather_kernel(received, total, dots):
+def gather_kernel(received, pieces, dots):
     value = received[0, :HEAD, :]
     for slot in range(1, NB):
         value = value + received[slot, :HEAD, :]
-    total[...] = value[:CHUNK]
-    dots[...] = value[CHUNK:]
+    for device in range(pieces.shape[0]):
+        pieces[device] = value[:PIECE]
+    dots[...] = value[PIECE:]
 
 
 def column_dot(pairs_of):
@@ -191,8 +238,11 @@
     groups, peers, counts, others, received, y, totals, cih, cil, high, low, scale,
     m, n, coarse, pair,
 ):
-    for rows in tiles():
-        put_split(pair, rows, totals[rows, :])
+    for device in range(totals.shape[0]):
+        first = (device % NCB) * CHUNK + (device // NCB) * PIECE
+        coarse[first : first + PIECE, :] = totals[device]
+    for rows in tiles():
+        put_split(pair, rows, coarse[rows, :])
     for rows in tiles():
         coarse[rows, :] = product(cih, cil, pair, rows)
 
@@ -224,7 +274,7 @@
 ):
     lanes = lax.broadcasted_iota(jnp.int32, (1, RHS), 1)
     for corner in range(NCB):
-        row = received[peers[0, (NB - NCB + corner) // 2], CHUNK : CHUNK + 1, :]
+        row = received[peers[0, (NB - NCB + corner) // 2], PIECE : PIECE + 1, :]
         picked = jnp.sum(jnp.where(lanes == corner, row, 0.0))
         others[0, corner] = picked.astype(jnp.int32)
     apply_all(
@@ -317,12 +367,12 @@
 
 FIELD = ((DOF, RHS), F32)
 MATRIX = ((DOF, DOF), BF16)
-HALF_BINS = ((4, HEAD, RHS), F32)
+HALF_BINS = ((4, CHUNK + EXTRA, RHS), F32)
 SMALL = ((EXTRA, RHS), F32)
 PAIR = pltpu.VMEM((DOF, 2 * RHS), BF16)
 PAIRS = pltpu.VMEM((2, DOF, 2 * RHS), BF16)
 FIELD_SCRATCH = pltpu.VMEM((DOF, RHS), F32)
-BINS = pltpu.VMEM((NCB, HEAD, RHS), F32)
+BINS = pltpu.VMEM((NCB, CHUNK + EXTRA, RHS), F32)
 STEP_FLOPS = 2 * DOF * DOF * RHS * 3
 
 
@@ -341,45 +391,61 @@
     b = right_side.reshape(DOF, RHS)
     place = lax.axis_index("corner").astype(jnp.int32).reshape(1)
     whole_inverse = lax.all_gather(coarse_inverse, "corner", axis=0, tiled=True)
-    group_row = jnp.zeros((EXTRA, RHS), F32).at[0, :NCB].set(corner_group[0].astype(F32))
     scale = jnp.broadcast_to(diagonal.reshape(DOF, 1), (DOF, RHS))
 
     def exchange(array, bit):
         return lax.ppermute(array, "corner", [(i, i ^ bit) for i in range(corners)])
 
-    def precondition(source, away, keep, extra):
+    def middle(first, last, state):
+        return call(
+            functools.partial(chebyshev_middle, first, last), f"chebyshev_{first}", "vvvvvvv",
+            "vvv", [FIELD] * 3, [PAIRS], STEP_FLOPS * (last - first),
+        )(*state, scale, inverse, high, low)
+
+    def precondition(source, away, keep, with_groups):
         came1 = exchange(away, 1)
-        x, h, e = call(
-            chebyshev_first, "chebyshev_first", "vvvvv", "vvv", [FIELD] * 3, [PAIRS],
-            STEP_FLOPS * SPLIT,
+        state = call(
+            functools.partial(chebyshev_first, CUTS[1]), "chebyshev_first", "vvvvv", "vvv",
+            [FIELD] * 3, [PAIRS], STEP_FLOPS * CUTS[1],
         )(source, scale, inverse, high, low)
-        came2 = exchange(keep[2:] + came1[2:], 2)
-        came3 = exchange(keep[1:2] + came1[1:2] + came2[1:2], 4)
+        rest = keep[1:] + came1[1:]
+        rest, *state = lax.optimization_barrier((rest, *state))
+        came2 = exchange(rest[1:2], 2)
+        came3 = exchange(rest[0:1], 4)
+        came4 = exchange(rest[2:3], 6)
+        state = middle(CUTS[1], CUTS[2], state)
         y, send = call(
-            functools.partial(chebyshev_last, extra is not None), "chebyshev_last",
-            "svvvvvvvvvvvv", "vv", [FIELD, ((NB, SLOT, RHS), F32)],
-            [FIELD_SCRATCH, FIELD_SCRATCH, PAIRS], STEP_FLOPS * (DEGREE - 1 - SPLIT),
+            functools.partial(chebyshev_last, with_groups, CUTS[2]), "chebyshev_last",
+            "ssvvvvvvvvvvvv", "vv", [FIELD, ((NB, SLOT, RHS), F32)],
+            [FIELD_SCRATCH, FIELD_SCRATCH, PAIRS], STEP_FLOPS * (DEGREE - 1 - CUTS[2]),
         )(
-            neighbours, scale, inverse, high, low, x, h, e, keep, came1, came2, came3,
-            group_row,
+            neighbours, corner_group, scale, inverse, high, low, *state, keep, came1,
+            came2, came3, came4,
         )
         received = lax.all_to_all(send, "sub", 0, 0, tiled=True)
-        total, dots = call(
-            gather_kernel, "gather", "v", "vv", [((CHUNK, RHS), F32), SMALL]
+        pieces, dots = call(
+            gather_kernel, "gather", "v", "vv", [((devices, PIECE, RHS), F32), SMALL]
         )(received)
-        totals = lax.all_gather(total, "corner", axis=0, tiled=True)
+        if with_groups:
+            pieces, *_ = lax.optimization_barrier((pieces, cih, cil))
+        totals = lax.all_to_all(pieces, ("sub", "corner"), 0, 0, tiled=True)
         return received, y, totals, dots
 
-    away, keep = call(
-        restrict_kernel, "restrict", "ssv", "vv", [HALF_BINS] * 2, [BINS]
-    )(corner_group, place, b)
-    high, low, inverse = call(
-        build_kernel, "build", "svv", "vvv", [MATRIX, MATRIX, FIELD],
-        [pltpu.VMEM((DOF, DOF), F32)], STEP_FLOPS * 3,
-    )(column_index, stiffness, scale)
+    high, low, inverse, away, keep = call(
+        build_kernel, "build", "sssvvv", "vvvvv",
+        [MATRIX, MATRIX, FIELD, HALF_BINS, HALF_BINS],
+        [
+            pltpu.VMEM((NB // 2, BW, BLOCK, 2 * BLOCK), F32),
+            pltpu.VMEM((BLOCK, DOF), F32),
+            pltpu.VMEM((BLOCK, DOF), F32),
+            pltpu.SMEM((NB, BW), jnp.int32),
+            BINS,
+        ],
+        STEP_FLOPS * 3,
+    )(column_index, corner_group, place, stiffness, scale, b)
     cih, cil = call(split_kernel, "split", "v", "vv", [MATRIX, MATRIX])(whole_inverse)
 
-    received, y, totals, _ = precondition(b, away, keep, group_row)
+    received, y, totals, _ = precondition(b, away, keep, True)
     u0, w0, away, keep, others = call(
         stage0_kernel, "stage0", "ssssvvvvvvvvv", "vvvvs",
         [FIELD, FIELD, HALF_BINS, HALF_BINS, ((1, NCB), jnp.int32)],
@@ -388,7 +454,7 @@
         corner_group, place, neighbours, face_count, received, y, totals, cih, cil,
         high, low, scale, b,
     )
-    received, y, totals, dots = precondition(w0, away, keep, None)
+    received, y, totals, dots = precondition(w0, away, keep, False)
     m0, n0, u1, w1, away, keep, before = call(
         stage1_kernel, "stage1", "sssssvvvvvvvvvvvv", "vvvvvvv",
         [FIELD] * 4 + [HALF_BINS, HALF_BINS, SMALL],
@@ -397,7 +463,7 @@
         corner_group, place, neighbours, face_count, others, received, y, totals, cih, cil,
         high, low, scale, b, dots, u0, w0,
     )
-    received, y, totals, dots = precondition(w1, away, keep, None)
+    received, y, totals, dots = precondition(w1, away, keep, False)
     p, s, u2, w2, last, scalars = call(
         stage2_kernel, "stage2", "ssssvvvvvvvvvvvvvvvvv", "vvvvvv",
         [FIELD] * 4 + [((devices, 3, RHS), F32), SMALL],

time: 286 us -> 229 us (0.80)
  Pallas kernels: 75.6 us -> 45.7 us
  blocking collectives: 161 us -> 141 us
  waiting for transfers between devices: 13.1 us -> 0.71 us
  starting transfers between devices: 9.89 us -> 14.2 us
    all_to_all x0 -> x3, blocking collectives: none -> 62.2 us  [precondition(): totals = lax.all_to_all(pieces, ('sub', 'corner'), 0, 0, tiled=True)]
    all_gather x3 -> x0, blocking collectives: 47.2 us -> none  [precondition(): totals = lax.all_gather(total, 'corner', axis=0, tiled=True)]
    all_to_all x3, blocking collectives: 99.1 us -> 63.1 us  [precondition(): received = lax.all_to_all(send, 'sub', 0, 0, tiled=True)]
    pallas_call x16 -> x18, Pallas kernels: 75.6 us -> 45.7 us  [run(): pl.pallas_call(body, name=name, in_specs=[spec(k) for k in kinds], out_sp...]
    ppermute x9 -> x12, waiting for transfers between devices: 12.5 us -> 0.03 us  [exchange(): return lax.ppermute(array, 'corner', [(i, i ^ bit) for i in range(corners)])]
    ppermute x9 -> x12, starting transfers between devices: 9.85 us -> 14.1 us  [exchange(): return lax.ppermute(array, 'corner', [(i, i ^ bit) for i in range(corners)])]
    unnamed x47 -> x33, local copies, waits for them, and re-layouts: 5.89 us -> 8.15 us
  transfers between devices with their start and end apart: 10 -> 13, of which waited for: 4 -> 0; matrix products, arithmetic and copies ran while one was open for 1% -> 1% of each run, Pallas kernels for 13% -> 13%
where the time goes in v2:
time: 229 us; the launch traced here: 225 us
  blocking collectives  141 us (62%)
  Pallas kernels  45.7 us (20%)
  between operations  14.6 us (6%)
  starting transfers between devices  14.2 us (6%)
  local copies, waits for them, and re-layouts  9.16 us (4%)
    all_to_all x3, blocking collectives, precondition(): received = lax.all_to_all(send, 'sub', 0, 0, tiled=True)  63.1 us
    all_to_all x3, blocking collectives, precondition(): totals = lax.all_to_all(pieces, ('sub', 'corner'), 0, 0, tiled=True)  62.2 us
    pallas_call x18, Pallas kernels, run(): pl.pallas_call(body, name=name, in_specs=[spec(k) for k in kinds], out_sp...  45.7 us
    all_to_all x1, blocking collectives, on_device(): all_dots = lax.all_to_all(last, ('sub', 'corner'), 0, 0, tiled=True)  15.2 us
    ppermute x12, starting transfers between devices, exchange(): return lax.ppermute(array, 'corner', [(i, i ^ bit) for i in range(corners)])  14.1 us
    unnamed x33, local copies, waits for them, and re-layouts  8.15 us
  transfers between devices with their start and end apart: 13, of which 0 were waited for; matrix products, arithmetic and copies ran while one was open for 1% of the time, Pallas kernels for 13%

profile of v2, /device:TPU:1, one launch (start us, length us, event | category | flops | bytes accessed | tf_op | source)
XLA Modules:
  0.0 225.0 jit_solution(9827284487685266398)
XLA Ops:
  7.2 0.7 all-gather.2.cloned.1.call-update
  7.9 0.8 broadcast_in_dim.7
  8.7 0.8 copy.10.column
  9.4 0.2 broadcast_in_dim.8.scale
  9.6 1.0 copy-done.2
  10.7 0.7 copy-done.11
  11.3 1.2 copy-done.15
  12.6 2.8 %build.1 = (bf16[1024,1024]{1,0:T(8,128)(2,1)S(1)}, bf16[1024,1024]{1,0:T(8,128)(2,1)S(1)}, f32[1024,128]{1,0:T(8,128)S(1)}, f32[4,136,128]{2,1,0:T(8,128)S(1)}, f32[4,136,128]{2,1,0:T(8,128)S(1)}) custom-call(s32[16,3]{1,0:T(8,128)S(1)} %copy.10.column, s32[1,8]{1,0:T(1,128)S(1)} %copy-done.11, s32[1]{0:T(128)} %bitcast.place, ...), custom_call_target="tpu_custom_call" | custom-call | flops 2415919104 | bytes 4194304 | tf_op jit(solution)/shard_map/build/pallas_call | solution.py:49
  15.4 1.5 collective-permute-start
  16.9 1.4 chebyshev_first.3
  18.3 2.6 %collective-permute-start.3 = (f32[1,136,128]{2,1,0:T(8,128)S(1)}, f32[1,136,128]{2,1,0:T(8,128)S(1)}, u32[]{:S(2)}, u32[]{:S(2)}) collective-permute-start(f32[1,136,128]{2,1,0:T(8,128)S(1)} %get-tuple-element.146), channel_id=1, source_target_pairs={{0,6},{1,7},{2,4},{3,5},{4,2},{5,3},{6,0},{7,1},{8,14},{9,15},{10,... | collective-permute-start | bytes 208904 | tf_op jit(solution)/shard_map/ppermute | solution.py:397
  21.0 0.5 collective-permute-start.2
  21.5 0.3 collective-permute-start.1
  21.8 5.9 %chebyshev_1.3 = (f32[1024,128]{1,0:T(8,128)S(1)}, f32[1024,128]{1,0:T(8,128)S(1)}, f32[1024,128]{1,0:T(8,128)S(1)}) custom-call(f32[1024,128]{1,0:T(8,128)S(1)} %get-tuple-element.79.x0, f32[1024,128]{1,0:T(8,128)S(1)} %get-tuple-element.80.h0, f32[1024,128]{1,0:T(8,128)S(1)} %get-tuple-element.81.e0, f32[1024,128]{1,0:T(8,128)S(1)} %broadcast_in_dim.8.scale, ...), custom_call_target="tpu_custom_call" | custom-call | flops 4026531840 | bytes 4194304 | tf_op jit(solution)/shard_map/chebyshev_1/pallas_call | solution.py:49
  27.8 1.9 chebyshev_last.3
  29.8 24.4 %all_to_all.35.received = f32[16,144,128]{2,1,0:T(8,128)S(1)} all-to-all(f32[16,144,128]{2,1,0:T(8,128)S(1)} %get-tuple-element.86), channel_id=1, replica_groups=mesh['sub'=16,'corner'=8] {'sub'}, dimensions={0} | all-to-all | bytes 2359296 | tf_op jit(solution)/shard_map/all_to_all | solution.py:425
  54.1 0.6 gather.3
  54.8 1.0 copy-done.4
  55.8 0.8 copy-done.9
  56.6 2.2 copy-done.6
  58.8 0.6 split.1
  59.4 0.4 copy-done.10
  59.8 21.7 %all_to_all.36.totals = f32[128,8,128]{2,1,0:T(8,128)S(1)} all-to-all(f32[128,8,128]{2,1,0:T(8,128)S(1)} %copy-done.10), channel_id=1, replica_groups=mesh['sub'=16,'corner'=8] {'sub','corner'}, dimensions={0} | all-to-all | bytes 1048576 | tf_op jit(solution)/shard_map/all_to_all | solution.py:431
  81.5 3.8 %stage0.1 = (f32[1024,128]{1,0:T(8,128)S(1)}, f32[1024,128]{1,0:T(8,128)S(1)}, f32[4,136,128]{2,1,0:T(8,128)S(1)}, f32[4,136,128]{2,1,0:T(8,128)S(1)}, s32[1,8]{1,0:T(1,128)S(1)}) custom-call(s32[1,8]{1,0:T(1,128)S(1)} %copy-done.12, s32[1]{0:T(128)} %bitcast.place, s32[1,8]{1,0:T(1,128)S(1)} %copy-done.13, s32[1,8]{1,0:T(1,128)S(1)} %copy-done.14, ...), custom_call_target="tpu_custom_call" | custom-call | flops 1610612736 | bytes 4194304 | tf_op jit(solution)/shard_map/stage0/pallas_call | solution.py:49
  85.3 1.4 collective-permute-start.4
  86.7 1.5 chebyshev_first.4
  88.2 0.6 collective-permute-start.7
  88.8 1.6 collective-permute-start.6
  90.4 1.2 collective-permute-start.5
  91.6 6.5 %chebyshev_1.4 = (f32[1024,128]{1,0:T(8,128)S(1)}, f32[1024,128]{1,0:T(8,128)S(1)}, f32[1024,128]{1,0:T(8,128)S(1)}) custom-call(f32[1024,128]{1,0:T(8,128)S(1)} %get-tuple-element.99.x0, f32[1024,128]{1,0:T(8,128)S(1)} %get-tuple-element.100.h0, f32[1024,128]{1,0:T(8,128)S(1)} %get-tuple-element.101.e0, f32[1024,128]{1,0:T(8,128)S(1)} %broadcast_in_dim.8.scale, ...), custom_call_target="tpu_custom_call" | custom-call | flops 4026531840 | bytes 4194304 | tf_op jit(solution)/shard_map/chebyshev_1/pallas_call | solution.py:49
  98.1 2.0 chebyshev_last.4
  100.1 19.4 %all_to_all.37.received = f32[16,144,128]{2,1,0:T(8,128)S(1)} all-to-all(f32[16,144,128]{2,1,0:T(8,128)S(1)} %get-tuple-element.106), channel_id=1, replica_groups=mesh['sub'=16,'corner'=8] {'sub'}, dimensions={0} | all-to-all | bytes 2359296 | tf_op jit(solution)/shard_map/all_to_all | solution.py:425
  119.5 0.1 gather.4
  119.6 20.3 %all_to_all.38.totals = f32[128,8,128]{2,1,0:T(8,128)S(1)} all-to-all(f32[128,8,128]{2,1,0:T(8,128)S(1)} %get-tuple-element.108), channel_id=1, replica_groups=mesh['sub'=16,'corner'=8] {'sub','corner'}, dimensions={0} | all-to-all | bytes 1048576 | tf_op jit(solution)/shard_map/all_to_all | solution.py:431
  139.8 3.6 %stage1.1 = (f32[1024,128]{1,0:T(8,128)S(1)}, f32[1024,128]{1,0:T(8,128)S(1)}, f32[1024,128]{1,0:T(8,128)S(1)}, f32[1024,128]{1,0:T(8,128)S(1)}, f32[4,136,128]{...) custom-call(s32[1,8]{1,0:T(1,128)S(1)} %copy-done.12, s32[1]{0:T(128)} %bitcast.place, ...), custom_call_target="tpu_custom_call" | custom-call | flops 1610612736 | bytes 4194304 | tf_op jit(solution)/shard_map/stage1/pallas_call | solution.py:49
  143.4 1.0 collective-permute-start.8
  144.4 1.5 chebyshev_first.5
  145.9 0.6 collective-permute-start.11
  146.5 1.6 collective-permute-start.10
  148.1 1.3 collective-permute-start.9
  149.4 6.5 %chebyshev_1.5 = (f32[1024,128]{1,0:T(8,128)S(1)}, f32[1024,128]{1,0:T(8,128)S(1)}, f32[1024,128]{1,0:T(8,128)S(1)}) custom-call(f32[1024,128]{1,0:T(8,128)S(1)} %get-tuple-element.117.x0, f32[1024,128]{1,0:T(8,128)S(1)} %get-tuple-element.118.h0, f32[1024,128]{1,0:T(8,128)S(1)} %get-tuple-element.119.e0, f32[1024,128]{1,0:T(8,128)S(1)} %broadcast_in_dim.8.scale, ...), custom_call_target="tpu_custom_call" | custom-call | flops 4026531840 | bytes 4194304 | tf_op jit(solution)/shard_map/chebyshev_1/pallas_call | solution.py:49
  155.9 2.0 chebyshev_last.5
  158.0 19.4 %all_to_all.39.received = f32[16,144,128]{2,1,0:T(8,128)S(1)} all-to-all(f32[16,144,128]{2,1,0:T(8,128)S(1)} %get-tuple-element.124), channel_id=1, replica_groups=mesh['sub'=16,'corner'=8] {'sub'}, dimensions={0} | all-to-all | bytes 2359296 | tf_op jit(solution)/shard_map/all_to_all | solution.py:425
  177.3 0.1 gather.5
  177.4 20.3 %all_to_all.40.totals = f32[128,8,128]{2,1,0:T(8,128)S(1)} all-to-all(f32[128,8,128]{2,1,0:T(8,128)S(1)} %get-tuple-element.126), channel_id=1, replica_groups=mesh['sub'=16,'corner'=8] {'sub','corner'}, dimensions={0} | all-to-all | bytes 1048576 | tf_op jit(solution)/shard_map/all_to_all | solution.py:431
  197.7 3.7 %stage2.1 = (f32[1024,128]{1,0:T(8,128)S(1)}, f32[1024,128]{1,0:T(8,128)S(1)}, f32[1024,128]{1,0:T(8,128)S(1)}, f32[1024,128]{1,0:T(8,128)S(1)}, f32[128,3,128]{2,1,0:T(4,128)S(1)}, /*index=5*/f32[8,128]{1,0:T(8,128)S(1)}) custom-call(s32[1,8]{1,0:T(1,128)S(1)} %copy-done.12, s32[1,8]{1,0:T(1,128)S(1)} %copy-done.13, s32[1,8]{1,0:T(1,128)S(1)} %copy-done.14, ...), custom_call_target="tpu_custom_call" | custom-call | flops 1610612736 | bytes 4194304 | tf_op jit(solution)/shard_map/stage2/pallas_call | solution.py:49
  201.4 15.2 %all_to_all.41.all_dots = f32[128,3,128]{2,1,0:T(4,128)S(1)} all-to-all(f32[128,3,128]{2,1,0:T(4,128)S(1)} %get-tuple-element.132), channel_id=1, replica_groups=mesh['sub'=16,'corner'=8] {'sub','corner'}, dimensions={0} | all-to-all | bytes 393216 | tf_op jit(solution)/shard_map/all_to_all | solution.py:475
  216.6 1.3 finish.1
  (45 shorter events, 0.3 us)
Async XLA Ops:
  7.2 49.4 %all-gather.2.cloned.1.call-start = ((), (), s32[]{:S(2)}) async-start(), calls=%async_computation.7 | async-start | bytes 4718592 | tf_op jit(solution)/shard_map/all_gather | solution.py:393
  9.6 1.0 copy-start.2
  10.7 0.7 copy-start.11
  11.3 1.2 copy-start.15
  15.4 12.4 %copy-start = (bf16[1024,1024]{1,0:T(8,128)(2,1)}, bf16[1024,1024]{1,0:T(8,128)(2,1)S(1)}, u32[]{:S(2)}) copy-start(bf16[1024,1024]{1,0:T(8,128)(2,1)S(1)} %get-tuple-element.73.low) | copy-start | bytes 6291460
  15.4 2.9 %collective-permute-start = (f32[4,136,128]{2,1,0:T(8,128)S(1)}, f32[4,136,128]{2,1,0:T(8,128)S(1)}, u32[]{:S(2)}, u32[]{:S(2)}) collective-permute-start(f32[4,136,128]{2,1,0:T(8,128)S(1)} %get-tuple-element.75), channel_id=1, source_target_pairs={{0,1},{1,0},{2,3},{3,2},{4,5},{5,4},{6,7},{7,6},{8,9},{9,8},{10,11... | collective-permute-start | bytes 835592 | tf_op jit(solution)/shard_map/ppermute | solution.py:397
  18.3 9.4 %collective-permute-start.3 = (f32[1,136,128]{2,1,0:T(8,128)S(1)}, f32[1,136,128]{2,1,0:T(8,128)S(1)}, u32[]{:S(2)}, u32[]{:S(2)}) collective-permute-start(f32[1,136,128]{2,1,0:T(8,128)S(1)} %get-tuple-element.146), channel_id=1, source_target_pairs={{0,6},{1,7},{2,4},{3,5},{4,2},{5,3},{6,0},{7,1},{8,14},{9,15},{10,... | collective-permute-start | bytes 208904 | tf_op jit(solution)/shard_map/ppermute | solution.py:397
  21.0 6.8 %collective-permute-start.2 = (f32[1,136,128]{2,1,0:T(8,128)S(1)}, f32[1,136,128]{2,1,0:T(8,128)S(1)}, u32[]{:S(2)}, u32[]{:S(2)}) collective-permute-start(f32[1,136,128]{2,1,0:T(8,128)S(1)} %get-tuple-element.147), channel_id=1, source_target_pairs={{0,4},{1,5},{2,6},{3,7},{4,0},{5,1},{6,2},{7,3},{8,12},{9,13},{10,... | collective-permute-start | bytes 208904 | tf_op jit(solution)/shard_map/ppermute | solution.py:397
  21.5 6.3 %copy-start.12 = (s32[1,8]{1,0:T(1,128)S(1)}, s32[1,8]{1,0:T(1,128)}, u32[]{:S(2)}) copy-start(s32[1,8]{1,0:T(1,128)} %groups.13) | copy-start | bytes 100
  21.5 6.3 %copy-start.13 = (s32[1,8]{1,0:T(1,128)S(1)}, s32[1,8]{1,0:T(1,128)}, u32[]{:S(2)}) copy-start(s32[1,8]{1,0:T(1,128)} %peers.11) | copy-start | bytes 100
  21.5 6.3 %collective-permute-start.1 = (f32[1,136,128]{2,1,0:T(8,128)S(1)}, f32[1,136,128]{2,1,0:T(8,128)S(1)}, u32[]{:S(2)}, u32[]{:S(2)}) collective-permute-start(f32[1,136,128]{2,1,0:T(8,128)S(1)} %get-tuple-element.148), channel_id=1, source_target_pairs={{0,2},{1,3},{2,0},{3,1},{4,6},{5,7},{6,4},{7,5},{8,10},{9,11},{10,... | collective-permute-start | bytes 208904 | tf_op jit(solution)/shard_map/ppermute | solution.py:397
  29.8 24.4 %copy-start.7 = (f32[1024,128]{1,0:T(8,128)}, f32[1024,128]{1,0:T(8,128)S(1)}, u32[]{:S(2)}) copy-start(f32[1024,128]{1,0:T(8,128)S(1)} %get-tuple-element.87.y) | copy-start | bytes 1572868
  54.8 1.0 copy-start.4
  55.8 0.8 copy-start.9
  56.6 2.2 copy-start.6
  58.8 1.0 copy-start.10
  58.8 22.7 %copy-start.1 = (bf16[1024,1024]{1,0:T(8,128)(2,1)S(1)}, bf16[1024,1024]{1,0:T(8,128)(2,1)}, u32[]{:S(2)}) copy-start(bf16[1024,1024]{1,0:T(8,128)(2,1)} %copy-done) | copy-start | bytes 6291460
  58.8 22.7 %copy-start.5 = (f32[16,144,128]{2,1,0:T(8,128)S(1)}, f32[16,144,128]{2,1,0:T(8,128)}, u32[]{:S(2)}) copy-start(f32[16,144,128]{2,1,0:T(8,128)} %copy-done.4) | copy-start | bytes 3538948
  58.8 22.7 %copy-start.14 = (s32[1,8]{1,0:T(1,128)S(1)}, s32[1,8]{1,0:T(1,128)}, u32[]{:S(2)}) copy-start(s32[1,8]{1,0:T(1,128)} %counts.5) | copy-start | bytes 100
  59.3 22.1 %copy-start.3 = (f32[16,64,128]{2,1,0:T(8,128)S(1)}, f32[16,64,128]{2,1,0:T(8,128)}, u32[]{:S(2)}) copy-start(f32[16,64,128]{2,1,0:T(8,128)} %param.8) | copy-start | bytes 1572868
  59.4 22.1 %copy-start.8 = (f32[1024,128]{1,0:T(8,128)S(1)}, f32[1024,128]{1,0:T(8,128)}, u32[]{:S(2)}) copy-start(f32[1024,128]{1,0:T(8,128)} %copy-done.7) | copy-start | bytes 1572868
  85.3 2.8 %collective-permute-start.4 = (f32[4,136,128]{2,1,0:T(8,128)S(1)}, f32[4,136,128]{2,1,0:T(8,128)S(1)}, u32[]{:S(2)}, u32[]{:S(2)}) collective-permute-start(f32[4,136,128]{2,1,0:T(8,128)S(1)} %get-tuple-element.94), channel_id=1, source_target_pairs={{0,1},{1,0},{2,3},{3,2},{4,5},{5,4},{6,7},{7,6},{8,9},{9,8},{10,11... | collective-permute-start | bytes 835592 | tf_op jit(solution)/shard_map/ppermute | solution.py:397
  88.2 9.8 %collective-permute-start.7 = (f32[1,136,128]{2,1,0:T(8,128)S(1)}, f32[1,136,128]{2,1,0:T(8,128)S(1)}, u32[]{:S(2)}, u32[]{:S(2)}) collective-permute-start(f32[1,136,128]{2,1,0:T(8,128)S(1)} %get-tuple-element.143), channel_id=1, source_target_pairs={{0,6},{1,7},{2,4},{3,5},{4,2},{5,3},{6,0},{7,1},{8,14},{9,15},{10,... | collective-permute-start | bytes 208904 | tf_op jit(solution)/shard_map/ppermute | solution.py:397
  88.8 9.3 %collective-permute-start.6 = (f32[1,136,128]{2,1,0:T(8,128)S(1)}, f32[1,136,128]{2,1,0:T(8,128)S(1)}, u32[]{:S(2)}, u32[]{:S(2)}) collective-permute-start(f32[1,136,128]{2,1,0:T(8,128)S(1)} %get-tuple-element.144), channel_id=1, source_target_pairs={{0,4},{1,5},{2,6},{3,7},{4,0},{5,1},{6,2},{7,3},{8,12},{9,13},{10,... | collective-permute-start | bytes 208904 | tf_op jit(solution)/shard_map/ppermute | solution.py:397
  90.4 7.7 %collective-permute-start.5 = (f32[1,136,128]{2,1,0:T(8,128)S(1)}, f32[1,136,128]{2,1,0:T(8,128)S(1)}, u32[]{:S(2)}, u32[]{:S(2)}) collective-permute-start(f32[1,136,128]{2,1,0:T(8,128)S(1)} %get-tuple-element.145), channel_id=1, source_target_pairs={{0,2},{1,3},{2,0},{3,1},{4,6},{5,7},{6,4},{7,5},{8,10},{9,11},{10,... | collective-permute-start | bytes 208904 | tf_op jit(solution)/shard_map/ppermute | solution.py:397
  143.4 2.4 %collective-permute-start.8 = (f32[4,136,128]{2,1,0:T(8,128)S(1)}, f32[4,136,128]{2,1,0:T(8,128)S(1)}, u32[]{:S(2)}, u32[]{:S(2)}) collective-permute-start(f32[4,136,128]{2,1,0:T(8,128)S(1)} %get-tuple-element.112), channel_id=1, source_target_pairs={{0,1},{1,0},{2,3},{3,2},{4,5},{5,4},{6,7},{7,6},{8,9},{9,8},{10,11... | collective-permute-start | bytes 835592 | tf_op jit(solution)/shard_map/ppermute | solution.py:397
  145.9 10.0 %collective-permute-start.11 = (f32[1,136,128]{2,1,0:T(8,128)S(1)}, f32[1,136,128]{2,1,0:T(8,128)S(1)}, u32[]{:S(2)}, u32[]{:S(2)}) collective-permute-start(f32[1,136,128]{2,1,0:T(8,128)S(1)} %get-tuple-element.140), channel_id=1, source_target_pairs={{0,6},{1,7},{2,4},{3,5},{4,2},{5,3},{6,0},{7,1},{8,14},{9,15},{10,... | collective-permute-start | bytes 208904 | tf_op jit(solution)/shard_map/ppermute | solution.py:397
  146.5 9.4 %collective-permute-start.10 = (f32[1,136,128]{2,1,0:T(8,128)S(1)}, f32[1,136,128]{2,1,0:T(8,128)S(1)}, u32[]{:S(2)}, u32[]{:S(2)}) collective-permute-start(f32[1,136,128]{2,1,0:T(8,128)S(1)} %get-tuple-element.141), channel_id=1, source_target_pairs={{0,4},{1,5},{2,6},{3,7},{4,0},{5,1},{6,2},{7,3},{8,12},{9,13},{10,... | collective-permute-start | bytes 208904 | tf_op jit(solution)/shard_map/ppermute | solution.py:397
  148.1 7.9 %collective-permute-start.9 = (f32[1,136,128]{2,1,0:T(8,128)S(1)}, f32[1,136,128]{2,1,0:T(8,128)S(1)}, u32[]{:S(2)}, u32[]{:S(2)}) collective-permute-start(f32[1,136,128]{2,1,0:T(8,128)S(1)} %get-tuple-element.142), channel_id=1, source_target_pairs={{0,2},{1,3},{2,0},{3,1},{4,6},{5,7},{6,4},{7,5},{8,10},{9,11},{10,... | collective-permute-start | bytes 208904 | tf_op jit(solution)/shard_map/ppermute | solution.py:397
Sparse Core Ops, SparseCore 0:
  9.7 36.0 all-gather.1
